TPU v7x, 512 devices: a whole 4x8x8 slice. The times are simulated.
512 devices in a mesh: wide: 128 (over z, y, core), sub: 4 (over x).
Axes of the slice: x: 4, y: 8, z: 8, core: 2. Of those that a mesh axis runs over, the one named last changes fastest.
Arguments:
- embeddings: bfloat16 [65536, 1024], P(('wide', 'sub'))
- cluster_ids: int32 [65536], P(('wide', 'sub')), may hold values from 0 to 6143, as said below
Outputs:
- nearest: float32 [65536], P(('wide', 'sub'))
Inputs may be any that keep to these rules, and one draw needn't show every extreme that they name: `cluster_ids`: cluster c belongs to owner c // 48 (an index along wide). Among the 128 documents of one device, at most 2 lie in clusters of one owner; in every draw some owner has exactly 2 such documents from every device. A cluster holds at most 44 documents, and some cluster holds exactly that many.
All inputs are finite; a program needn't handle non-finite values.
Results may differ from a plain program's by a relative error of at most 0.00047.
Values may be sent and summed in bfloat16 or wider, within the bound.
No kernel may reach another device: no remote copies, remote signals or barrier semaphores. Data moves between devices by JAX's collectives and lax.ppermute only.
A program may use at most 64 MiB of HBM per device.

v0:
```python
import jax
import jax.numpy as jnp
from jax import lax
from jax.sharding import PartitionSpec as P

CL_DEV = 48


EPSILON = 1e-06


def raw_scores(query_rows, key_rows):
    return lax.dot_general(
        query_rows, key_rows, (((1,), (1,)), ((), ())), preferred_element_type=jnp.float32
    )


def apply_mask(scores, query_meta, key_meta, along):
    allowed = (query_meta[0][:, None] == key_meta[0][None, :]) & (
        key_meta[1][None, :] < query_meta[1][:, None]
    )
    return jnp.max(jnp.where(allowed, scores, jnp.float32(-1.0)), axis=along)


def flatten_meta(meta):
    return (meta[:, 0, :].reshape(-1), meta[:, 1, :].reshape(-1))


def per_device(embeddings, cluster_ids):
    doc_count, width = embeddings.shape
    wide_count = lax.axis_size("wide")
    sub_count = lax.axis_size("sub")
    capacity = max(2, 2 * doc_count // wide_count)
    total_slots = wide_count * capacity
    values = embeddings.astype(jnp.float32)
    unit_rows = (
        values * lax.rsqrt(jnp.sum(values * values, axis=1, keepdims=True) + EPSILON)
    ).astype(jnp.bfloat16)
    owner_idx = cluster_ids // CL_DEV
    one_hot = (owner_idx[:, None] == jnp.arange(wide_count, dtype=jnp.int32)[None, :]).astype(
        jnp.int32
    )
    slot_rank = jnp.sum((jnp.cumsum(one_hot, axis=0) - one_hot) * one_hot, axis=1)
    slot_index = owner_idx * capacity + slot_rank
    device_row = lax.axis_index("wide") * sub_count + lax.axis_index("sub")
    positions = device_row * doc_count + jnp.arange(doc_count, dtype=jnp.int32)
    send_rows = jnp.zeros((total_slots, width), jnp.bfloat16).at[slot_index].set(unit_rows)
    send_rows = send_rows.reshape(wide_count, capacity, width)
    send_labels = jnp.full((total_slots,), -1, jnp.int32).at[slot_index].set(cluster_ids)
    send_places = jnp.full((total_slots,), -1, jnp.int32).at[slot_index].set(positions)
    send_meta = jnp.stack(
        [send_labels.reshape(wide_count, capacity), send_places.reshape(wide_count, capacity)],
        axis=1,
    )
    recv_rows, recv_meta = (
        lax.all_to_all(send_rows, "wide", split_axis=0, concat_axis=0, tiled=True),
        lax.all_to_all(send_meta, "wide", split_axis=0, concat_axis=0, tiled=True),
    )
    query_rows = recv_rows.reshape(-1, width)
    query_meta = flatten_meta(recv_meta)
    initial = jnp.full((total_slots,), -1.0, jnp.float32)
    key_rows = lax.all_gather(recv_rows, "sub", axis=0, tiled=True).reshape(-1, width)
    scores = raw_scores(query_rows, key_rows)
    nearest = jnp.maximum(
        initial,
        apply_mask(
            scores,
            query_meta,
            flatten_meta(lax.all_gather(recv_meta, "sub", axis=0, tiled=True)),
            1,
        ),
    )
    answer = lax.all_to_all(
        nearest.reshape(wide_count, capacity), "wide", split_axis=0, concat_axis=0, tiled=True
    )
    return answer.reshape(-1)[slot_index]


def solution(mesh):
    in_specs = (P(("wide", "sub"), None), P(("wide", "sub")))
    out_specs = P(("wide", "sub"))
    return jax.shard_map(
        per_device, mesh=mesh, in_specs=in_specs, out_specs=out_specs, check_vma=False
    )
```

profile of v0, /device:TPU:1, one launch (start us, length us, event | category | flops | bytes accessed | tf_op | source)
XLA Modules:
  0.0 119.4 jit_solution(328928367140373133)
XLA Ops:
  6.5 0.0 all-gather.2.cloned.1.call-start
  6.5 0.7 and_select_fusion
  7.2 0.1 fusion.7
  7.3 0.2 reduce_window_sum.11
  7.5 0.2 select_reduce_fusion
  7.6 1.1 fusion.1
  8.7 0.7 compare_select_fusion
  9.4 1.8 %scatter_custom_fusion.2 = bf16[256,1024]{1,0:T(8,128)(2,1)S(1)} fusion(s32[128]{0:T(128)S(1)} %get-tuple-element.9, bf16[128,1024]{1,0:T(8,128)(2,1)} %param.2, f32[128]{0:T(128)S(1)} %add_rsqrt_fusion, bf16[]{:T(256)} %constant.41.clone.1), kind=kCustom, calls=%fused_computation.10 | custom fusion | flops 393216 | bytes 786946 | tf_op jit(solution)/shard_map/scatter | solution.py:47
  11.2 0.2 reshape.40
  11.4 38.9 %all_to_all.16 = bf16[128,2,1024]{2,1,0:T(2,128)(2,1)} all-to-all(bf16[128,2,1024]{2,1,0:T(2,128)(2,1)S(1)} %reshape.40), channel_id=1, replica_groups=mesh['wide'=128,'sub'=4] {'wide'}, dimensions={0} | all-to-all | bytes 1048576 | tf_op jit(solution)/shard_map/all_to_all | solution.py:56
  50.3 0.0 copy-start
  50.3 0.0 all-gather.2.cloned.1.call-update
  50.4 1.2 %scatter_custom_fusion = s32[256]{0:T(256)S(1)} fusion(s32[128]{0:T(128)S(1)} %get-tuple-element.9, s32[128]{0:T(128)} %param.3, s32[]{:T(128)} %constant.16.clone.1), kind=kCustom, calls=%fused_computation.27 | custom fusion | bytes 1536 | tf_op jit(solution)/shard_map/scatter | solution.py:49
  51.6 1.0 scatter_custom_fusion.1
  52.6 0.1 stack_reshape.7
  52.7 0.1 stack_reshape.6
  52.9 0.1 copy.14
  53.0 17.9 %all_to_all.17 = s32[128,2,2]{2,1,0:T(2,128)S(1)} all-to-all(s32[128,2,2]{2,1,0:T(2,128)S(1)} %copy.14), channel_id=1, replica_groups=mesh['wide'=128,'sub'=4] {'wide'}, dimensions={0} | all-to-all | bytes 4096 | tf_op jit(solution)/shard_map/all_to_all | solution.py:57
  70.9 0.1 copy.15
  71.0 8.3 %all_gather.6 = s32[512,2,2]{0,2,1:T(2,128)S(1)} all-gather(s32[128,2,2]{0,2,1:T(2,128)S(1)} %copy.15), channel_id=1, replica_groups=mesh['wide'=128,'sub'=4] {'sub'}, dimensions={0}, use_global_device_ids=true | all-gather | bytes 10240 | tf_op jit(solution)/shard_map/all_gather | solution.py:69
  79.3 0.1 copy.17
  79.4 0.2 lt.24
  79.6 0.1 copy.16
  79.8 0.2 eq.35
  79.9 0.4 slice_reduce_fusion.1
  80.3 0.1 lt.26
  80.4 0.1 eq.33
  80.6 0.0 copy-done
  80.6 0.2 reshape.41
  80.8 0.0 all-gather.2.cloned.1.call-done
  80.8 2.8 %reshape.42 = bf16[1024,1024]{1,0:T(8,128)(2,1)S(1)} reshape(bf16[512,2,1024]{2,1,0:T(2,128)(2,1)} %all-gather.2.cloned.1.call-done) | data formatting | bytes 4194304 | tf_op jit(solution)/shard_map/reshape | solution.py:62
  83.6 0.9 fusion
  84.5 0.8 max_broadcast_in_dim.15
  85.2 12.7 %all-to-all-start.2 = ((f32[128,1,2]{2,1,0:T(1,128)}), f32[128,1,2]{2,1,0:T(1,128)S(1)}, u32[]{:S(2)}, u32[]{:S(2)}) async-start(f32[128,1,2]{2,1,0:T(1,128)} %bitcast), calls=%async_computation.2 | async-start | bytes 131072 | tf_op jit(solution)/shard_map/all_to_all | solution.py:73
  97.9 11.4 %all-to-all-done.2 = f32[128,1,2]{2,1,0:T(1,128)S(1)} async-done(((f32[128,1,2]{2,1,0:T(1,128)}), f32[128,1,2]{2,1,0:T(1,128)S(1)}, u32[]{:S(2)}, u32[]{:S(2)}) %all-to-all-start.2) | async-done | bytes 1056 | tf_op jit(solution)/shard_map/all_to_all | solution.py:73
  109.4 0.5 broadcast.49
  109.9 0.8 reduce.11
  110.7 0.1 reshape.43
  110.8 1.8 %gather_fusion = f32[128]{0:T(128)} fusion(f32[256]{0:T(256)S(1)} %reshape.43, s32[1024]{0:T(1024)S(1)} %pad_clamp_fusion), kind=kCustom, calls=%fused_computation | custom fusion | bytes 1536 | tf_op jit(solution)/shard_map/gather | solution.py:76
  (5 shorter events, 0.0 us)
Async XLA Ops:
  6.5 74.3 %all-gather.2.cloned.1.call-start = ((), (), s32[]{:S(2)}) async-start(), calls=%async_computation.3 | async-start | bytes 2621440 | tf_op jit(solution)/shard_map/all_gather | solution.py:62
  50.3 30.3 %copy-start = (bf16[128,2,1024]{2,1,0:T(2,128)(2,1)S(1)}, bf16[128,2,1024]{2,1,0:T(2,128)(2,1)}, u32[]{:S(2)}) copy-start(bf16[128,2,1024]{2,1,0:T(2,128)(2,1)} %all_to_all.16) | copy-start | bytes 1572868
  85.2 24.1 %all-to-all-start.2 = ((f32[128,1,2]{2,1,0:T(1,128)}), f32[128,1,2]{2,1,0:T(1,128)S(1)}, u32[]{:S(2)}, u32[]{:S(2)}) async-start(f32[128,1,2]{2,1,0:T(1,128)} %bitcast), calls=%async_computation.2 | async-start | bytes 131072 | tf_op jit(solution)/shard_map/all_to_all | solution.py:73
Sparse Core Ops, SparseCore 0:
  50.5 28.6 all-gather.1
where the time goes:
time: 120 us; the launch traced here: 119 us
  blocking collectives  65.1 us (54%)
  between operations  13.6 us (11%)
  starting transfers between devices  12.7 us (11%)
  waiting for transfers between devices  11.5 us (10%)
  local copies, waits for them, and re-layouts  10.3 us (9%)
  other arithmetic  5.48 us (5%)
    all_to_all x1, blocking collectives, per_device(): lax.all_to_all(send_rows, 'wide', split_axis=0, concat_axis=0, tiled=True)  38.9 us
    all_to_all x1, blocking collectives, per_device(): lax.all_to_all(send_meta, 'wide', split_axis=0, concat_axis=0, tiled=True)  17.9 us
    all_to_all x1, starting transfers between devices, per_device(): lax.all_to_all(nearest.reshape(wide_count, capacity), 'wide', split_axis=...  12.7 us
    all_to_all x1, waiting for transfers between devices, per_device(): lax.all_to_all(nearest.reshape(wide_count, capacity), 'wide', split_axis=...  11.4 us
    all_gather x1, blocking collectives, per_device(): lax.all_gather(recv_meta, 'sub', axis=0, tiled=True)  8.26 us
    reshape x1, local copies, waits for them, and re-layouts, per_device(): lax.all_gather(recv_rows, 'sub', axis=0, tiled=True).reshape(-1, width)  2.75 us
  transfers between devices with their start and end apart: 2, of which 1 were waited for; matrix products, arithmetic and copies ran while one was open for 3% of the time, Pallas kernels for 0%

commit v1 on v0

v1 whole, which is shorter than its diff:
```python
import jax
import jax.numpy as jnp
from jax import lax
from jax.sharding import Mesh, PartitionSpec as P

CL_DEV = 48
EPSILON = 1e-06
META = 128
AXES = ("chip", "core", "far", "near")
PEERS = ("chip", "near")


def swap(value, axis):
    return lax.ppermute(value, axis, [(0, 1), (1, 0)])


def order_of(count, core, far):
    slot = lax.iota(jnp.int32, count)
    peer, rank = slot // 2, slot % 2
    device = (((peer // 2) * 2 + core) * 2 + far) * 2 + peer % 2
    return device * 2 + rank


def best(query, query_meta, key, key_meta):
    scores = lax.dot_general(
        query, key, (((1,), (1,)), ((), ())), preferred_element_type=jnp.float32
    )
    allowed = (query_meta[0][:, None] == key_meta[0][None, :]) & (
        key_meta[1][None, :] < query_meta[1][:, None]
    )
    return jnp.max(jnp.where(allowed, scores, jnp.float32(-1.0)), axis=1)


def per_device(embeddings, cluster_ids):
    docs, width = embeddings.shape
    peers = lax.axis_size("chip") * lax.axis_size("near")
    slots = 2 * peers
    values = embeddings.astype(jnp.float32)
    unit = (
        values * lax.rsqrt(jnp.sum(values * values, axis=1, keepdims=True) + EPSILON)
    ).astype(jnp.bfloat16)
    owner = cluster_ids // CL_DEV
    label = (cluster_ids - owner * CL_DEV + 1).astype(jnp.bfloat16)
    place = lax.iota(jnp.int32, docs)
    twin = (owner[:, None] == owner[None, :]) & (place[None, :] < place[:, None])
    slot = owner * 2 + jnp.any(twin, axis=1).astype(jnp.int32)
    pick = slot[None, :] == lax.broadcasted_iota(jnp.int32, (slots, docs), 0)
    payload = jnp.concatenate(
        [unit, jnp.broadcast_to(label[:, None], (docs, META))], axis=1
    )
    send = lax.dot_general(
        pick.astype(jnp.bfloat16),
        payload,
        (((1,), (0,)), ((), ())),
        preferred_element_type=jnp.float32,
    ).astype(jnp.bfloat16)
    recv = lax.all_to_all(
        send.reshape(peers, 2, width + META), PEERS, split_axis=0, concat_axis=0, tiled=True
    ).reshape(slots, width + META)
    rows, mark = recv[:, :width], recv[:, width]
    core, far = lax.axis_index("core"), lax.axis_index("far")
    far_rows, far_mark = swap(rows, "far"), swap(mark, "far")
    core_rows, core_mark = swap(rows, "core"), swap(mark, "core")
    both_rows, both_mark = swap(far_rows, "core"), swap(far_mark, "core")
    mine = (mark, order_of(slots, core, far))
    nearest = best(rows, mine, rows, mine)
    for key, key_mark, c, f in (
        (core_rows, core_mark, 1 - core, far),
        (far_rows, far_mark, core, 1 - far),
        (both_rows, both_mark, 1 - core, 1 - far),
    ):
        found = best(rows, mine, key, (key_mark, order_of(slots, c, f)))
        nearest = jnp.maximum(nearest, found)
    answer = lax.all_to_all(
        nearest.reshape(peers, 2), PEERS, split_axis=0, concat_axis=0, tiled=True
    ).reshape(-1)
    return jnp.sum(jnp.where(pick, answer[:, None], jnp.float32(0.0)), axis=0)


def solution(mesh):
    fine = Mesh(mesh.devices.reshape(mesh.shape["wide"] // 2, 2, 2, 2), AXES)
    return jax.shard_map(
        per_device,
        mesh=fine,
        in_specs=(P(AXES, None), P(AXES)),
        out_specs=P(AXES),
        check_vma=False,
    )
```

time: 120 us -> 87.2 us (0.73)
  between operations: 13.6 us -> 0.19 us
  waiting for transfers between devices: 11.5 us -> 0.35 us
  local copies, waits for them, and re-layouts: 10.3 us -> 1.47 us
  starting transfers between devices: 12.7 us -> 21.4 us
  blocking collectives: 65.1 us -> 57.2 us
    ppermute x0 -> x6, starting transfers between devices: none -> 21.4 us  [swap(): return lax.ppermute(value, axis, [(0, 1), (1, 0)])]
    all_to_all x1 -> x0, starting transfers between devices: 12.7 us -> none  [per_device(): lax.all_to_all(nearest.reshape(wide_count, capacity), 'wide', split_axis=...]
    all_to_all x1 -> x0, waiting for transfers between devices: 11.4 us -> none  [per_device(): lax.all_to_all(nearest.reshape(wide_count, capacity), 'wide', split_axis=...]
    all_gather x1 -> x0, blocking collectives: 8.26 us -> none  [per_device(): lax.all_gather(recv_meta, 'sub', axis=0, tiled=True)]
    reshape x4 -> x2, local copies, waits for them, and re-layouts: 3.28 us -> 0.44 us  [the longest x1 0.22 us: per_device(): send.reshape(peers, 2, width + META)]
    scatter x2 -> x0, local copies, waits for them, and re-layouts: 2.21 us -> none  [the longest x1 1.24 us: per_device(): jnp.full((total_slots,), -1, jnp.int32).at[slot_index].set(cluster_ids)]
    scatter x1 -> x0, other arithmetic: 1.79 us -> none  [per_device(): jnp.zeros((total_slots, width), jnp.bfloat16).at[slot_index].set(unit_rows)]
    gather x1 -> x0, local copies, waits for them, and re-layouts: 1.77 us -> none  [per_device(): return answer.reshape(-1)[slot_index]]
  transfers between devices with their start and end apart: 2 -> 6, of which waited for: 1 -> 1; matrix products, arithmetic and copies ran while one was open for 3% -> 1% of each run, Pallas kernels for 0% -> 0%
where the time goes in v1:
time: 87.2 us; the launch traced here: 86.8 us
  blocking collectives  57.2 us (66%)
  starting transfers between devices  21.4 us (25%)
  other arithmetic  4.49 us (5%)
  matrix products  1.74 us (2%)
  local copies, waits for them, and re-layouts  1.47 us (2%)
    all_to_all x1, blocking collectives, per_device(): lax.all_to_all(send.reshape(peers, 2, width + META), PEERS, split_axis=0,...  37 us
    ppermute x6, starting transfers between devices, swap(): return lax.ppermute(value, axis, [(0, 1), (1, 0)])  21.4 us
    all_to_all x1, blocking collectives, per_device(): lax.all_to_all(nearest.reshape(peers, 2), PEERS, split_axis=0, concat_axi...  20.2 us
  transfers between devices with their start and end apart: 6, of which 1 were waited for; matrix products, arithmetic and copies ran while one was open for 1% of the time, Pallas kernels for 0%

profile of v1, /device:TPU:1, one launch (start us, length us, event | category | flops | bytes accessed | tf_op | source)
XLA Modules:
  0.0 86.8 jit_solution(6052062378998249516)
XLA Ops:
  0.0 0.7 add_convert_fusion
  0.7 0.2 fusion.8
  0.9 1.1 %fusion.1 = f32[128]{0:T(128)S(1)} fusion(bf16[128,1024]{1,0:T(8,128)(2,1)} %param.2), kind=kLoop, calls=%fused_computation.5 | loop fusion | flops 393088 | bytes 262656 | tf_op jit(solution)/shard_map/reduce_sum | solution.py:40
  2.0 1.1 %fusion.2 = bf16[128,1024]{1,0:T(8,128)(2,1)S(1)} fusion(bf16[128,1024]{1,0:T(8,128)(2,1)} %param.2, f32[128]{0:T(128)S(1)} %add_rsqrt_fusion), kind=kLoop, calls=%fused_computation.6 | loop fusion | flops 393216 | bytes 524800 | tf_op jit(solution)/shard_map/convert_element_type | solution.py:41
  3.0 0.1 broadcast_in_dim.19
  3.1 0.3 convolution_convert_fusion
  3.4 0.2 reshape.200
  3.7 37.0 %all_to_all.11 = bf16[128,2,1152]{2,1,0:T(2,128)(2,1)S(1)} all-to-all(bf16[128,2,1152]{2,1,0:T(2,128)(2,1)S(1)} %reshape.200), channel_id=1, replica_groups=mesh['chip'=64,'core'=2,'far'=2,'near'=2] {'chip','near'}, dimensions={0} | all-to-all | bytes 1179648 | tf_op jit(solution)/shard_map/all_to_all | solution.py:57
  40.6 0.2 reshape.201
  40.9 0.1 slice.9
  40.9 4.4 %collective-permute-start.3 = (bf16[256,1024]{1,0:T(8,128)(2,1)S(1)}, bf16[256,1024]{1,0:T(8,128)(2,1)S(1)}, u32[]{:S(2)}, u32[]{:S(2)}) collective-permute-start(bf16[256,1024]{1,0:T(8,128)(2,1)S(1)} %slice.9), channel_id=1, source_target_pairs={{0,2},{2,0},{1,3},{3,1},{4,6},{6,4},{5,7},{7,5},{8,10},{10,8},{9,1... | collective-permute-start | bytes 1572872 | tf_op jit(solution)/shard_map/ppermute | solution.py:14
  45.3 6.0 %collective-permute-start.1 = (bf16[256,1024]{1,0:T(8,128)(2,1)S(1)}, bf16[256,1024]{1,0:T(8,128)(2,1)S(1)}, u32[]{:S(2)}, u32[]{:S(2)}) collective-permute-start(bf16[256,1024]{1,0:T(8,128)(2,1)S(1)} %slice.9), channel_id=1, source_target_pairs={{0,4},{4,0},{1,5},{5,1},{2,6},{6,2},{3,7},{7,3},{8,12},{12,8},{9,1... | collective-permute-start | bytes 1572872 | tf_op jit(solution)/shard_map/ppermute | solution.py:14
  51.4 0.1 slice_reduce_fusion
  51.5 1.9 %collective-permute-start = (bf16[256]{0:T(256)(128)(2,1)S(1)}, bf16[256]{0:T(256)(128)(2,1)S(1)}, u32[]{:S(2)}, u32[]{:S(2)}) collective-permute-start(bf16[256]{0:T(256)(128)(2,1)S(1)} %slice_reduce_fusion), channel_id=1, source_target_pairs={{0,4},{4,0},{1,5},{5,1},{2,6},{6,2},{3,7},{7,3},{8,12},{12,8},{9,1... | collective-permute-start | bytes 1544 | tf_op jit(solution)/shard_map/ppermute | solution.py:14
  53.4 2.4 %collective-permute-start.2 = (bf16[256]{0:T(256)(128)(2,1)S(1)}, bf16[256]{0:T(256)(128)(2,1)S(1)}, u32[]{:S(2)}, u32[]{:S(2)}) collective-permute-start(bf16[256]{0:T(256)(128)(2,1)S(1)} %slice_reduce_fusion), channel_id=1, source_target_pairs={{0,2},{2,0},{1,3},{3,1},{4,6},{6,4},{5,7},{7,5},{8,10},{10,8},{9,1... | collective-permute-start | bytes 1544 | tf_op jit(solution)/shard_map/ppermute | solution.py:14
  55.9 0.0 collective-permute-done.3
  55.9 4.7 %collective-permute-start.5 = (bf16[256,1024]{1,0:T(8,128)(2,1)S(1)}, bf16[256,1024]{1,0:T(8,128)(2,1)S(1)}, u32[]{:S(2)}, u32[]{:S(2)}) collective-permute-start(bf16[256,1024]{1,0:T(8,128)(2,1)S(1)} %collective-permute-done.3), channel_id=1, source_target_pairs={{0,4},{4,0},{1,5},{5,1},{2,6},{6,2},{3,7},{7,3},{8,12},{12,8},{9,1... | collective-permute-start | bytes 1572872 | tf_op jit(solution)/shard_map/ppermute | solution.py:14
  60.6 0.3 fusion
  60.9 0.0 collective-permute-done.2
  60.9 1.9 %collective-permute-start.4 = (bf16[256]{0:T(256)(128)(2,1)S(1)}, bf16[256]{0:T(256)(128)(2,1)S(1)}, u32[]{:S(2)}, u32[]{:S(2)}) collective-permute-start(bf16[256]{0:T(256)(128)(2,1)S(1)} %collective-permute-done.2), channel_id=1, source_target_pairs={{0,4},{4,0},{1,5},{5,1},{2,6},{6,2},{3,7},{7,3},{8,12},{12,8},{9,1... | collective-permute-start | bytes 1544 | tf_op jit(solution)/shard_map/ppermute | solution.py:14
  62.9 0.4 select_reduce_fusion.1
  63.2 0.0 collective-permute-done
  63.2 0.0 collective-permute-done.1
  63.3 0.4 select_reduce_fusion.2
  63.6 0.3 collective-permute-done.4
  64.0 0.0 collective-permute-done.5
  64.0 0.4 select_reduce_fusion
  64.3 0.1 max.41
  64.5 20.2 %all_to_all.12 = f32[128,1,2]{2,1,0:T(1,128)S(1)} all-to-all(f32[128,1,2]{2,1,0:T(1,128)S(1)} %bitcast.4), channel_id=1, replica_groups=mesh['chip'=64,'core'=2,'far'=2,'near'=2] {'chip','near'}, dimensions={0} | all-to-all | bytes 2048 | tf_op jit(solution)/shard_map/all_to_all | solution.py:74
  84.7 0.5 broadcast.553
  85.2 0.8 reduce.5
  86.1 0.1 broadcast_in_dim.21
  86.2 0.6 select_reduce_fusion.3
  (5 shorter events, 0.1 us)
Async XLA Ops:
  40.9 14.9 %collective-permute-start.3 = (bf16[256,1024]{1,0:T(8,128)(2,1)S(1)}, bf16[256,1024]{1,0:T(8,128)(2,1)S(1)}, u32[]{:S(2)}, u32[]{:S(2)}) collective-permute-start(bf16[256,1024]{1,0:T(8,128)(2,1)S(1)} %slice.9), channel_id=1, source_target_pairs={{0,2},{2,0},{1,3},{3,1},{4,6},{6,4},{5,7},{7,5},{8,10},{10,8},{9,1... | collective-permute-start | bytes 1572872 | tf_op jit(solution)/shard_map/ppermute | solution.py:14
  45.3 17.9 %collective-permute-start.1 = (bf16[256,1024]{1,0:T(8,128)(2,1)S(1)}, bf16[256,1024]{1,0:T(8,128)(2,1)S(1)}, u32[]{:S(2)}, u32[]{:S(2)}) collective-permute-start(bf16[256,1024]{1,0:T(8,128)(2,1)S(1)} %slice.9), channel_id=1, source_target_pairs={{0,4},{4,0},{1,5},{5,1},{2,6},{6,2},{3,7},{7,3},{8,12},{12,8},{9,1... | collective-permute-start | bytes 1572872 | tf_op jit(solution)/shard_map/ppermute | solution.py:14
  51.5 11.7 %collective-permute-start = (bf16[256]{0:T(256)(128)(2,1)S(1)}, bf16[256]{0:T(256)(128)(2,1)S(1)}, u32[]{:S(2)}, u32[]{:S(2)}) collective-permute-start(bf16[256]{0:T(256)(128)(2,1)S(1)} %slice_reduce_fusion), channel_id=1, source_target_pairs={{0,4},{4,0},{1,5},{5,1},{2,6},{6,2},{3,7},{7,3},{8,12},{12,8},{9,1... | collective-permute-start | bytes 1544 | tf_op jit(solution)/shard_map/ppermute | solution.py:14
  53.4 7.5 %collective-permute-start.2 = (bf16[256]{0:T(256)(128)(2,1)S(1)}, bf16[256]{0:T(256)(128)(2,1)S(1)}, u32[]{:S(2)}, u32[]{:S(2)}) collective-permute-start(bf16[256]{0:T(256)(128)(2,1)S(1)} %slice_reduce_fusion), channel_id=1, source_target_pairs={{0,2},{2,0},{1,3},{3,1},{4,6},{6,4},{5,7},{7,5},{8,10},{10,8},{9,1... | collective-permute-start | bytes 1544 | tf_op jit(solution)/shard_map/ppermute | solution.py:14
  55.9 8.1 %collective-permute-start.5 = (bf16[256,1024]{1,0:T(8,128)(2,1)S(1)}, bf16[256,1024]{1,0:T(8,128)(2,1)S(1)}, u32[]{:S(2)}, u32[]{:S(2)}) collective-permute-start(bf16[256,1024]{1,0:T(8,128)(2,1)S(1)} %collective-permute-done.3), channel_id=1, source_target_pairs={{0,4},{4,0},{1,5},{5,1},{2,6},{6,2},{3,7},{7,3},{8,12},{12,8},{9,1... | collective-permute-start | bytes 1572872 | tf_op jit(solution)/shard_map/ppermute | solution.py:14
  60.9 3.0 %collective-permute-start.4 = (bf16[256]{0:T(256)(128)(2,1)S(1)}, bf16[256]{0:T(256)(128)(2,1)S(1)}, u32[]{:S(2)}, u32[]{:S(2)}) collective-permute-start(bf16[256]{0:T(256)(128)(2,1)S(1)} %collective-permute-done.2), channel_id=1, source_target_pairs={{0,4},{4,0},{1,5},{5,1},{2,6},{6,2},{3,7},{7,3},{8,12},{12,8},{9,1... | collective-permute-start | bytes 1544 | tf_op jit(solution)/shard_map/ppermute | solution.py:14

commit v2 on v1

v2 whole, which is shorter than its diff:
```python
import jax
import jax.numpy as jnp
from jax import lax
from jax.sharding import Mesh, PartitionSpec as P

CL_DEV = 48
EPSILON = 1e-06
META = 128
AXES = ("chip", "core", "far", "near")
PEERS = ("chip", "near")
EVERY = ("far", "chip", "near")


def order_of(count, core):
    slot = lax.iota(jnp.int32, count)
    rank, near, rest = slot % 2, slot // 2 % 2, slot // 4
    chips = lax.axis_size("chip")
    device = ((rest % chips * 2 + core) * 2 + rest // chips) * 2 + near
    return device * 2 + rank


def best(query, query_meta, key, key_meta):
    scores = lax.dot_general(
        query, key, (((1,), (1,)), ((), ())), preferred_element_type=jnp.float32
    )
    allowed = (query_meta[0][:, None] == key_meta[0][None, :]) & (
        key_meta[1][None, :] < query_meta[1][:, None]
    )
    return jnp.max(jnp.where(allowed, scores, jnp.float32(-1.0)), axis=1)


def per_device(embeddings, cluster_ids):
    docs, width = embeddings.shape
    owners = lax.axis_size("chip") * lax.axis_size("near")
    slots = 2 * owners
    values = embeddings.astype(jnp.float32)
    unit = (
        values * lax.rsqrt(jnp.sum(values * values, axis=1, keepdims=True) + EPSILON)
    ).astype(jnp.bfloat16)
    owner = cluster_ids // CL_DEV
    label = (cluster_ids - owner * CL_DEV + 1).astype(jnp.bfloat16)
    place = lax.iota(jnp.int32, docs)
    twin = (owner[:, None] == owner[None, :]) & (place[None, :] < place[:, None])
    slot = owner * 2 + jnp.any(twin, axis=1).astype(jnp.int32)
    pick = slot[None, :] == lax.broadcasted_iota(jnp.int32, (slots, docs), 0)
    payload = jnp.concatenate(
        [unit, jnp.broadcast_to(label[:, None], (docs, META))], axis=1
    )
    twice = jnp.concatenate([pick, pick], axis=0).astype(jnp.bfloat16)
    send = lax.dot_general(
        twice, payload, (((1,), (0,)), ((), ())), preferred_element_type=jnp.float32
    ).astype(jnp.bfloat16)
    rows = lax.all_to_all(
        send.reshape(2 * owners, 2, width + META), EVERY, split_axis=0, concat_axis=0, tiled=True
    ).reshape(2 * slots, width + META)
    other = lax.ppermute(rows, "core", [(0, 1), (1, 0)])
    core, far = lax.axis_index("core"), lax.axis_index("far")
    query = lax.dynamic_slice_in_dim(rows, far * slots, slots, 0)
    order = order_of(2 * slots, core)
    query_meta = (query[:, width], lax.dynamic_slice_in_dim(order, far * slots, slots, 0))
    here = best(query[:, :width], query_meta, rows[:, :width], (rows[:, width], order))
    there = best(
        query[:, :width],
        query_meta,
        other[:, :width],
        (other[:, width], order_of(2 * slots, 1 - core)),
    )
    nearest = jnp.maximum(here, there)
    answer = lax.all_to_all(
        nearest.reshape(owners, 2), PEERS, split_axis=0, concat_axis=0, tiled=True
    ).reshape(-1)
    return jnp.sum(jnp.where(pick, answer[:, None], jnp.float32(0.0)), axis=0)


def solution(mesh):
    fine = Mesh(mesh.devices.reshape(mesh.shape["wide"] // 2, 2, 2, 2), AXES)
    return jax.shard_map(
        per_device,
        mesh=fine,
        in_specs=(P(AXES, None), P(AXES)),
        out_specs=P(AXES),
        check_vma=False,
    )
```

time: 87.2 us -> 87.2 us (level)
  starting transfers between devices: 21.4 us -> 4.66 us
  blocking collectives: 57.2 us -> 72.3 us
  waiting for transfers between devices: 0.35 us -> 1.52 us
    ppermute x6 -> x1, starting transfers between devices: 21.4 us -> 4.66 us  [per_device(): other = lax.ppermute(rows, 'core', [(0, 1), (1, 0)])]
    all_to_all x2, blocking collectives: 57.2 us -> 72.3 us  [the longest x1 55.4 us: per_device(): lax.all_to_all(send.reshape(2 * owners, 2, width + META), EVERY, split_ax...]
    ppermute x6 -> x1, waiting for transfers between devices: 0.35 us -> 1.52 us  [per_device(): other = lax.ppermute(rows, 'core', [(0, 1), (1, 0)])]
  transfers between devices with their start and end apart: 6 -> 1, of which waited for: 1 -> 1; matrix products, arithmetic and copies ran while one was open for 1% -> 1% of each run, Pallas kernels for 0% -> 0%
where the time goes in v2:
time: 87.2 us; the launch traced here: 86.9 us
  blocking collectives  72.3 us (83%)
  starting transfers between devices  4.66 us (5%)
  other arithmetic  4.5 us (5%)
  local copies, waits for them, and re-layouts  2.26 us (3%)
  matrix products  1.6 us (2%)
  waiting for transfers between devices  1.52 us (2%)
    all_to_all x1, blocking collectives, per_device(): lax.all_to_all(send.reshape(2 * owners, 2, width + META), EVERY, split_ax...  55.4 us
    all_to_all x1, blocking collectives, per_device(): lax.all_to_all(nearest.reshape(owners, 2), PEERS, split_axis=0, concat_ax...  16.9 us
    ppermute x1, starting transfers between devices, per_device(): other = lax.ppermute(rows, 'core', [(0, 1), (1, 0)])  4.66 us
  transfers between devices with their start and end apart: 1, of which 1 were waited for; matrix products, arithmetic and copies ran while one was open for 1% of the time, Pallas kernels for 0%

profile of v2, /device:TPU:1, one launch (start us, length us, event | category | flops | bytes accessed | tf_op | source)
XLA Modules:
  0.0 86.9 jit_solution(18239773956443759497)
XLA Ops:
  0.0 0.7 add_convert_fusion
  0.7 1.1 %fusion.4 = f32[128]{0:T(128)S(1)} fusion(bf16[128,1024]{1,0:T(8,128)(2,1)} %param.2), kind=kLoop, calls=%fused_computation.8 | loop fusion | flops 393088 | bytes 262656 | tf_op jit(solution)/shard_map/reduce_sum | solution.py:38
  1.8 1.1 %fusion.5 = bf16[128,1024]{1,0:T(8,128)(2,1)S(1)} fusion(bf16[128,1024]{1,0:T(8,128)(2,1)} %param.2, f32[128]{0:T(128)S(1)} %add_rsqrt_fusion), kind=kLoop, calls=%fused_computation.9 | loop fusion | flops 393216 | bytes 524800 | tf_op jit(solution)/shard_map/convert_element_type | solution.py:39
  2.8 0.2 fusion.19
  3.1 0.1 broadcast_in_dim.17
  3.1 0.5 convolution_convert_fusion
  3.6 0.5 reshape.126
  4.1 55.4 %all_to_all.11 = bf16[256,2,1152]{2,1,0:T(2,128)(2,1)S(1)} all-to-all(bf16[256,2,1152]{2,1,0:T(2,128)(2,1)S(1)} %reshape.126), channel_id=1, replica_groups=mesh['chip'=64,'core'=2,'far'=2,'near'=2] {'far','chip','near'}, dimensions={0} | all-to-all | bytes 2359296 | tf_op jit(solution)/shard_map/all_to_all | solution.py:53
  59.5 0.5 reshape.127
  60.0 4.7 %collective-permute-start = (bf16[512,1152]{1,0:T(8,128)(2,1)S(1)}, bf16[512,1152]{1,0:T(8,128)(2,1)S(1)}, u32[]{:S(2)}, u32[]{:S(2)}) collective-permute-start(bf16[512,1152]{1,0:T(8,128)(2,1)S(1)} %reshape.127), channel_id=1, source_target_pairs={{0,4},{4,0},{1,5},{5,1},{2,6},{6,2},{3,7},{7,3},{8,12},{12,8},{9,1... | collective-permute-start | bytes 3538952 | tf_op jit(solution)/shard_map/ppermute | solution.py:56
  64.7 0.1 dynamic_slice.7
  64.8 0.1 dynamic-slice_reduce_fusion
  64.9 0.1 slice_reduce_fusion.1
  65.0 0.6 fusion
  65.6 1.5 %collective-permute-done = bf16[512,1152]{1,0:T(8,128)(2,1)S(1)} collective-permute-done((bf16[512,1152]{1,0:T(8,128)(2,1)S(1)}, bf16[512,1152]{1,0:T(8,128)(2,1)S(1)}, u32[]{:S(2)}, u32[]{:S(2)}) %collective-permute-start) | collective-permute-done | bytes 1179680 | tf_op jit(solution)/shard_map/ppermute | solution.py:56
  67.1 0.1 slice_reduce_fusion
  67.3 0.6 select_reduce_fusion
  67.8 0.1 max.15
  68.0 16.9 %all_to_all.12 = f32[128,1,2]{2,1,0:T(1,128)S(1)} all-to-all(f32[128,1,2]{2,1,0:T(1,128)S(1)} %bitcast.1), channel_id=1, replica_groups=mesh['chip'=64,'core'=2,'far'=2,'near'=2] {'chip','near'}, dimensions={0} | all-to-all | bytes 2048 | tf_op jit(solution)/shard_map/all_to_all | solution.py:69
  84.8 0.5 broadcast.347
  85.3 0.8 reduce.9
  86.2 0.1 broadcast_in_dim.19
  86.3 0.6 select_reduce_fusion.1
  (6 shorter events, 0.1 us)
Async XLA Ops:
  60.0 7.1 %collective-permute-start = (bf16[512,1152]{1,0:T(8,128)(2,1)S(1)}, bf16[512,1152]{1,0:T(8,128)(2,1)S(1)}, u32[]{:S(2)}, u32[]{:S(2)}) collective-permute-start(bf16[512,1152]{1,0:T(8,128)(2,1)S(1)} %reshape.127), channel_id=1, source_target_pairs={{0,4},{4,0},{1,5},{5,1},{2,6},{6,2},{3,7},{7,3},{8,12},{12,8},{9,1... | collective-permute-start | bytes 3538952 | tf_op jit(solution)/shard_map/ppermute | solution.py:56

commit v3 on v1

--- a/solution.py
+++ b/solution.py
@@ -1,6 +1,8 @@
 import jax
 import jax.numpy as jnp
 from jax import lax
+from jax.experimental import pallas as pl
+from jax.experimental.pallas import tpu as pltpu
 from jax.sharding import Mesh, PartitionSpec as P
 
 CL_DEV = 48
@@ -8,6 +10,48 @@
 META = 128
 AXES = ("chip", "core", "far", "near")
 PEERS = ("chip", "near")
+
+
+def place_kernel(ids_ref, emb_ref, out_ref, slot_ref):
+    docs, width = emb_ref.shape
+    slots = out_ref.shape[0]
+    ids = ids_ref[...]
+    owner = (ids * 43691) >> 21
+    label = (ids - owner * CL_DEV + 1).astype(jnp.float32)
+    slot = lax.broadcasted_iota(jnp.int32, (slots, docs), 0)
+    mine = (slot >> 1) == owner
+    square = (docs, docs)
+    earlier = lax.broadcasted_iota(jnp.int32, square, 0) < lax.broadcasted_iota(
+        jnp.int32, square, 1
+    )
+    seen = jnp.dot(
+        mine.astype(jnp.bfloat16), earlier.astype(jnp.bfloat16), preferred_element_type=jnp.float32
+    )
+    pick = mine & (seen == (slot & 1).astype(jnp.float32))
+    values = emb_ref[...].astype(jnp.float32)
+    unit = (
+        values * lax.rsqrt(jnp.sum(values * values, axis=1, keepdims=True) + EPSILON)
+    ).astype(jnp.bfloat16)
+    out_ref[:, :width] = jnp.dot(
+        pick.astype(jnp.bfloat16), unit, preferred_element_type=jnp.float32
+    ).astype(jnp.bfloat16)
+    mark = jnp.sum(jnp.where(pick, label, 0.0), axis=1, keepdims=True)
+    out_ref[:, width:] = jnp.broadcast_to(mark, (slots, META)).astype(jnp.bfloat16)
+    slot_ref[...] = jnp.sum(jnp.where(pick, slot, 0), axis=0, keepdims=True)
+
+
+def place(embeddings, cluster_ids, slots):
+    docs, width = embeddings.shape
+    return pl.pallas_call(
+        place_kernel,
+        out_shape=(
+            jax.ShapeDtypeStruct((slots, width + META), jnp.bfloat16),
+            jax.ShapeDtypeStruct((1, docs), jnp.int32),
+        ),
+        in_specs=[pl.BlockSpec(memory_space=pltpu.VMEM)] * 2,
+        out_specs=(pl.BlockSpec(memory_space=pltpu.VMEM),) * 2,
+        compiler_params=pltpu.CompilerParams(vmem_limit_bytes=16 * 1024 * 1024),
+    )(cluster_ids.reshape(1, docs), embeddings)
 
 
 def swap(value, axis):
@@ -35,25 +79,7 @@
     docs, width = embeddings.shape
     peers = lax.axis_size("chip") * lax.axis_size("near")
     slots = 2 * peers
-    values = embeddings.astype(jnp.float32)
-    unit = (
-        values * lax.rsqrt(jnp.sum(values * values, axis=1, keepdims=True) + EPSILON)
-    ).astype(jnp.bfloat16)
-    owner = cluster_ids // CL_DEV
-    label = (cluster_ids - owner * CL_DEV + 1).astype(jnp.bfloat16)
-    place = lax.iota(jnp.int32, docs)
-    twin = (owner[:, None] == owner[None, :]) & (place[None, :] < place[:, None])
-    slot = owner * 2 + jnp.any(twin, axis=1).astype(jnp.int32)
-    pick = slot[None, :] == lax.broadcasted_iota(jnp.int32, (slots, docs), 0)
-    payload = jnp.concatenate(
-        [unit, jnp.broadcast_to(label[:, None], (docs, META))], axis=1
-    )
-    send = lax.dot_general(
-        pick.astype(jnp.bfloat16),
-        payload,
-        (((1,), (0,)), ((), ())),
-        preferred_element_type=jnp.float32,
-    ).astype(jnp.bfloat16)
+    send, slot = place(embeddings, cluster_ids, slots)
     recv = lax.all_to_all(
         send.reshape(peers, 2, width + META), PEERS, split_axis=0, concat_axis=0, tiled=True
     ).reshape(slots, width + META)
@@ -72,9 +98,11 @@
         found = best(rows, mine, key, (key_mark, order_of(slots, c, f)))
         nearest = jnp.maximum(nearest, found)
     answer = lax.all_to_all(
-        nearest.reshape(peers, 2), PEERS, split_axis=0, concat_axis=0, tiled=True
-    ).reshape(-1)
-    return jnp.sum(jnp.where(pick, answer[:, None], jnp.float32(0.0)), axis=0)
+        nearest.reshape(peers, 1, 2), PEERS, split_axis=0, concat_axis=0, tiled=True
+    ).reshape(peers, 2)
+    chosen = jnp.where((slot & 1) == 0, answer[:, 0:1], answer[:, 1:2])
+    here = (slot >> 1) == lax.broadcasted_iota(jnp.int32, (peers, docs), 0)
+    return jnp.sum(jnp.where(here, chosen, jnp.float32(0.0)), axis=0)
 
 
 def solution(mesh):

time: 87.2 us -> 86.4 us (level)
  blocking collectives: 57.2 us -> 0 us
  starting transfers between devices: 21.4 us -> 50.2 us
  waiting for transfers between devices: 0.35 us -> 29 us
  other arithmetic: 4.49 us -> 0.7 us
  local copies, waits for them, and re-layouts: 1.47 us -> 3.95 us
    all_to_all x2 -> x0, blocking collectives: 57.2 us -> none  [the longest x1 37 us: per_device(): lax.all_to_all(send.reshape(peers, 2, width + META), PEERS, split_axis=0,...]
    all_to_all x0 -> x2, starting transfers between devices: none -> 28.9 us  [the longest x1 19.3 us: per_device(): lax.all_to_all(send.reshape(peers, 2, width + META), PEERS, split_axis=0,...]
    all_to_all x0 -> x2, waiting for transfers between devices: none -> 28.7 us  [the longest x1 17.9 us: per_device(): lax.all_to_all(send.reshape(peers, 2, width + META), PEERS, split_axis=0,...]
    convert_element_type x2 -> x0, other arithmetic: 1.74 us -> none  [the longest x1 1.07 us: per_device(): unit = (values * lax.rsqrt(jnp.sum(values * values, axis=1, keepdims=True...]
    unnamed x0 -> x4, local copies, waits for them, and re-layouts: none -> 1.6 us
    reduce_sum x2 -> x1, other arithmetic: 1.72 us -> 0.64 us  [per_device(): return jnp.sum(jnp.where(here, chosen, jnp.float32(0.0)), axis=0)]
  transfers between devices with their start and end apart: 6 -> 8, of which waited for: 1 -> 3; matrix products, arithmetic and copies ran while one was open for 1% -> 1% of each run, Pallas kernels for 0% -> 0%
where the time goes in v3:
time: 86.4 us; the launch traced here: 86 us
  starting transfers between devices  50.2 us (58%)
  waiting for transfers between devices  29 us (34%)
  local copies, waits for them, and re-layouts  3.95 us (5%)
  matrix products  1.46 us (2%)
    ppermute x6, starting transfers between devices, swap(): return lax.ppermute(value, axis, [(0, 1), (1, 0)])  21.4 us
    all_to_all x1, starting transfers between devices, per_device(): lax.all_to_all(send.reshape(peers, 2, width + META), PEERS, split_axis=0,...  19.3 us
    all_to_all x1, waiting for transfers between devices, per_device(): lax.all_to_all(send.reshape(peers, 2, width + META), PEERS, split_axis=0,...  17.9 us
    all_to_all x1, waiting for transfers between devices, per_device(): lax.all_to_all(nearest.reshape(peers, 1, 2), PEERS, split_axis=0, concat_...  10.8 us
    all_to_all x1, starting transfers between devices, per_device(): lax.all_to_all(nearest.reshape(peers, 1, 2), PEERS, split_axis=0, concat_...  9.58 us
  transfers between devices with their start and end apart: 8, of which 3 were waited for; matrix products, arithmetic and copies ran while one was open for 1% of the time, Pallas kernels for 0%

profile of v3, /device:TPU:1, one launch (start us, length us, event | category | flops | bytes accessed | tf_op | source)
XLA Modules:
  0.0 86.0 jit_solution(16245691519944007310)
XLA Ops:
  0.0 0.0 copy-start.1
  0.0 0.7 copy-done.1
  0.7 0.0 copy-start
  0.7 0.9 %copy-done = bf16[128,1024]{1,0:T(8,128)(2,1)S(1)} copy-done((bf16[128,1024]{1,0:T(8,128)(2,1)S(1)}, bf16[128,1024]{1,0:T(8,128)(2,1)}, u32[]{:S(2)}) %copy-start) | copy-done | bytes 262168
  1.6 0.4 shard_map.28
  2.0 1.0 %reshape.189 = bf16[128,2,1152]{2,1,0:T(2,128)(2,1)} reshape(bf16[256,1152]{1,0:T(8,128)(2,1)S(1)} %get-tuple-element.8) | data formatting | bytes 1179648 | tf_op jit(solution)/shard_map/reshape | solution.py:84
  3.1 19.3 %all-to-all-start = ((bf16[128,2,1152]{2,1,0:T(2,128)(2,1)}), bf16[128,2,1152]{2,1,0:T(2,128)(2,1)S(1)}, u32[]{:S(2)}, u32[]{:S(2)}) async-start(bf16[128,2,1152]{2,1,0:T(2,128)(2,1)} %reshape.189), calls=%async_computation | async-start | bytes 1179648 | tf_op jit(solution)/shard_map/all_to_all | solution.py:83
  22.4 17.9 %all-to-all-done = bf16[128,2,1152]{2,1,0:T(2,128)(2,1)S(1)} async-done(((bf16[128,2,1152]{2,1,0:T(2,128)(2,1)}), bf16[128,2,1152]{2,1,0:T(2,128)(2,1)S(1)}, u32[]{:S(2)}, u32[]{:S(2)}) %all-to-all-start) | async-done | bytes 589856 | tf_op jit(solution)/shard_map/all_to_all | solution.py:83
  40.3 0.2 reshape.190
  40.5 0.1 slice.17
  40.6 4.4 %collective-permute-start.3 = (bf16[256,1024]{1,0:T(8,128)(2,1)S(1)}, bf16[256,1024]{1,0:T(8,128)(2,1)S(1)}, u32[]{:S(2)}, u32[]{:S(2)}) collective-permute-start(bf16[256,1024]{1,0:T(8,128)(2,1)S(1)} %slice.17), channel_id=1, source_target_pairs={{0,2},{2,0},{1,3},{3,1},{4,6},{6,4},{5,7},{7,5},{8,10},{10,8},{9,1... | collective-permute-start | bytes 1572872 | tf_op jit(solution)/shard_map/ppermute | solution.py:58
  45.0 6.0 %collective-permute-start.1 = (bf16[256,1024]{1,0:T(8,128)(2,1)S(1)}, bf16[256,1024]{1,0:T(8,128)(2,1)S(1)}, u32[]{:S(2)}, u32[]{:S(2)}) collective-permute-start(bf16[256,1024]{1,0:T(8,128)(2,1)S(1)} %slice.17), channel_id=1, source_target_pairs={{0,4},{4,0},{1,5},{5,1},{2,6},{6,2},{3,7},{7,3},{8,12},{12,8},{9,1... | collective-permute-start | bytes 1572872 | tf_op jit(solution)/shard_map/ppermute | solution.py:58
  51.0 0.1 slice_reduce_fusion.2
  51.1 1.9 %collective-permute-start = (bf16[256]{0:T(256)(128)(2,1)S(1)}, bf16[256]{0:T(256)(128)(2,1)S(1)}, u32[]{:S(2)}, u32[]{:S(2)}) collective-permute-start(bf16[256]{0:T(256)(128)(2,1)S(1)} %slice_reduce_fusion.2), channel_id=1, source_target_pairs={{0,4},{4,0},{1,5},{5,1},{2,6},{6,2},{3,7},{7,3},{8,12},{12,8},{9,1... | collective-permute-start | bytes 1544 | tf_op jit(solution)/shard_map/ppermute | solution.py:58
  53.1 2.4 %collective-permute-start.2 = (bf16[256]{0:T(256)(128)(2,1)S(1)}, bf16[256]{0:T(256)(128)(2,1)S(1)}, u32[]{:S(2)}, u32[]{:S(2)}) collective-permute-start(bf16[256]{0:T(256)(128)(2,1)S(1)} %slice_reduce_fusion.2), channel_id=1, source_target_pairs={{0,2},{2,0},{1,3},{3,1},{4,6},{6,4},{5,7},{7,5},{8,10},{10,8},{9,1... | collective-permute-start | bytes 1544 | tf_op jit(solution)/shard_map/ppermute | solution.py:58
  55.5 0.0 collective-permute-done.3
  55.5 4.7 %collective-permute-start.5 = (bf16[256,1024]{1,0:T(8,128)(2,1)S(1)}, bf16[256,1024]{1,0:T(8,128)(2,1)S(1)}, u32[]{:S(2)}, u32[]{:S(2)}) collective-permute-start(bf16[256,1024]{1,0:T(8,128)(2,1)S(1)} %collective-permute-done.3), channel_id=1, source_target_pairs={{0,4},{4,0},{1,5},{5,1},{2,6},{6,2},{3,7},{7,3},{8,12},{12,8},{9,1... | collective-permute-start | bytes 1572872 | tf_op jit(solution)/shard_map/ppermute | solution.py:58
  60.2 0.4 fusion
  60.6 0.0 collective-permute-done.2
  60.6 1.9 %collective-permute-start.4 = (bf16[256]{0:T(256)(128)(2,1)S(1)}, bf16[256]{0:T(256)(128)(2,1)S(1)}, u32[]{:S(2)}, u32[]{:S(2)}) collective-permute-start(bf16[256]{0:T(256)(128)(2,1)S(1)} %collective-permute-done.2), channel_id=1, source_target_pairs={{0,4},{4,0},{1,5},{5,1},{2,6},{6,2},{3,7},{7,3},{8,12},{12,8},{9,1... | collective-permute-start | bytes 1544 | tf_op jit(solution)/shard_map/ppermute | solution.py:58
  62.5 0.4 select_reduce_fusion.1
  62.9 0.0 collective-permute-done
  62.9 0.0 collective-permute-done.1
  62.9 0.4 select_reduce_fusion.2
  63.3 0.3 collective-permute-done.4
  63.6 0.0 collective-permute-done.5
  63.6 0.4 select_reduce_fusion
  64.0 0.8 max.38
  64.7 9.6 %all-to-all-start.1 = ((f32[128,1,2]{2,1,0:T(1,128)}), f32[128,1,2]{2,1,0:T(1,128)S(1)}, u32[]{:S(2)}, u32[]{:S(2)}) async-start(f32[128,1,2]{2,1,0:T(1,128)} %bitcast.3), calls=%async_computation.1 | async-start | bytes 131072 | tf_op jit(solution)/shard_map/all_to_all | solution.py:100
  74.3 10.8 %all-to-all-done.1 = f32[128,1,2]{2,1,0:T(1,128)S(1)} async-done(((f32[128,1,2]{2,1,0:T(1,128)}), f32[128,1,2]{2,1,0:T(1,128)S(1)}, u32[]{:S(2)}, u32[]{:S(2)}) %all-to-all-start.1) | async-done | bytes 1056 | tf_op jit(solution)/shard_map/all_to_all | solution.py:100
  85.1 0.2 slice_reduce_fusion.1
  85.3 0.6 select_reduce_fusion.3
  (5 shorter events, 0.1 us)
Async XLA Ops:
  0.0 0.7 copy-start.1
  0.7 0.9 %copy-start = (bf16[128,1024]{1,0:T(8,128)(2,1)S(1)}, bf16[128,1024]{1,0:T(8,128)(2,1)}, u32[]{:S(2)}) copy-start(bf16[128,1024]{1,0:T(8,128)(2,1)} %emb_ref.1) | copy-start | bytes 786436
  3.1 37.2 %all-to-all-start = ((bf16[128,2,1152]{2,1,0:T(2,128)(2,1)}), bf16[128,2,1152]{2,1,0:T(2,128)(2,1)S(1)}, u32[]{:S(2)}, u32[]{:S(2)}) async-start(bf16[128,2,1152]{2,1,0:T(2,128)(2,1)} %reshape.189), calls=%async_computation | async-start | bytes 1179648 | tf_op jit(solution)/shard_map/all_to_all | solution.py:83
  40.6 15.0 %collective-permute-start.3 = (bf16[256,1024]{1,0:T(8,128)(2,1)S(1)}, bf16[256,1024]{1,0:T(8,128)(2,1)S(1)}, u32[]{:S(2)}, u32[]{:S(2)}) collective-permute-start(bf16[256,1024]{1,0:T(8,128)(2,1)S(1)} %slice.17), channel_id=1, source_target_pairs={{0,2},{2,0},{1,3},{3,1},{4,6},{6,4},{5,7},{7,5},{8,10},{10,8},{9,1... | collective-permute-start | bytes 1572872 | tf_op jit(solution)/shard_map/ppermute | solution.py:58
  45.0 17.9 %collective-permute-start.1 = (bf16[256,1024]{1,0:T(8,128)(2,1)S(1)}, bf16[256,1024]{1,0:T(8,128)(2,1)S(1)}, u32[]{:S(2)}, u32[]{:S(2)}) collective-permute-start(bf16[256,1024]{1,0:T(8,128)(2,1)S(1)} %slice.17), channel_id=1, source_target_pairs={{0,4},{4,0},{1,5},{5,1},{2,6},{6,2},{3,7},{7,3},{8,12},{12,8},{9,1... | collective-permute-start | bytes 1572872 | tf_op jit(solution)/shard_map/ppermute | solution.py:58
  51.1 11.7 %collective-permute-start = (bf16[256]{0:T(256)(128)(2,1)S(1)}, bf16[256]{0:T(256)(128)(2,1)S(1)}, u32[]{:S(2)}, u32[]{:S(2)}) collective-permute-start(bf16[256]{0:T(256)(128)(2,1)S(1)} %slice_reduce_fusion.2), channel_id=1, source_target_pairs={{0,4},{4,0},{1,5},{5,1},{2,6},{6,2},{3,7},{7,3},{8,12},{12,8},{9,1... | collective-permute-start | bytes 1544 | tf_op jit(solution)/shard_map/ppermute | solution.py:58
  53.1 7.5 %collective-permute-start.2 = (bf16[256]{0:T(256)(128)(2,1)S(1)}, bf16[256]{0:T(256)(128)(2,1)S(1)}, u32[]{:S(2)}, u32[]{:S(2)}) collective-permute-start(bf16[256]{0:T(256)(128)(2,1)S(1)} %slice_reduce_fusion.2), channel_id=1, source_target_pairs={{0,2},{2,0},{1,3},{3,1},{4,6},{6,4},{5,7},{7,5},{8,10},{10,8},{9,1... | collective-permute-start | bytes 1544 | tf_op jit(solution)/shard_map/ppermute | solution.py:58
  55.5 8.1 %collective-permute-start.5 = (bf16[256,1024]{1,0:T(8,128)(2,1)S(1)}, bf16[256,1024]{1,0:T(8,128)(2,1)S(1)}, u32[]{:S(2)}, u32[]{:S(2)}) collective-permute-start(bf16[256,1024]{1,0:T(8,128)(2,1)S(1)} %collective-permute-done.3), channel_id=1, source_target_pairs={{0,4},{4,0},{1,5},{5,1},{2,6},{6,2},{3,7},{7,3},{8,12},{12,8},{9,1... | collective-permute-start | bytes 1572872 | tf_op jit(solution)/shard_map/ppermute | solution.py:58
  60.6 3.0 %collective-permute-start.4 = (bf16[256]{0:T(256)(128)(2,1)S(1)}, bf16[256]{0:T(256)(128)(2,1)S(1)}, u32[]{:S(2)}, u32[]{:S(2)}) collective-permute-start(bf16[256]{0:T(256)(128)(2,1)S(1)} %collective-permute-done.2), channel_id=1, source_target_pairs={{0,4},{4,0},{1,5},{5,1},{2,6},{6,2},{3,7},{7,3},{8,12},{12,8},{9,1... | collective-permute-start | bytes 1544 | tf_op jit(solution)/shard_map/ppermute | solution.py:58
  64.7 20.4 %all-to-all-start.1 = ((f32[128,1,2]{2,1,0:T(1,128)}), f32[128,1,2]{2,1,0:T(1,128)S(1)}, u32[]{:S(2)}, u32[]{:S(2)}) async-start(f32[128,1,2]{2,1,0:T(1,128)} %bitcast.3), calls=%async_computation.1 | async-start | bytes 131072 | tf_op jit(solution)/shard_map/all_to_all | solution.py:100

commit v4 on v3

--- a/solution.py
+++ b/solution.py
@@ -10,6 +10,8 @@
 META = 128
 AXES = ("chip", "core", "far", "near")
 PEERS = ("chip", "near")
+VMEM = pl.BlockSpec(memory_space=pltpu.VMEM)
+ROOM = pltpu.CompilerParams(vmem_limit_bytes=16 * 1024 * 1024)
 
 
 def place_kernel(ids_ref, emb_ref, out_ref, slot_ref):
@@ -48,10 +50,29 @@
             jax.ShapeDtypeStruct((slots, width + META), jnp.bfloat16),
             jax.ShapeDtypeStruct((1, docs), jnp.int32),
         ),
-        in_specs=[pl.BlockSpec(memory_space=pltpu.VMEM)] * 2,
-        out_specs=(pl.BlockSpec(memory_space=pltpu.VMEM),) * 2,
-        compiler_params=pltpu.CompilerParams(vmem_limit_bytes=16 * 1024 * 1024),
+        in_specs=[VMEM, VMEM],
+        out_specs=(VMEM, VMEM),
+        compiler_params=ROOM,
     )(cluster_ids.reshape(1, docs), embeddings)
+
+
+def take_kernel(slot_ref, answer_ref, out_ref):
+    slot = slot_ref[...]
+    answer = answer_ref[...]
+    owners = answer.shape[0]
+    chosen = jnp.where((slot & 1) == 0, answer[:, 0:1], answer[:, 1:2])
+    here = (slot >> 1) == lax.broadcasted_iota(jnp.int32, (owners, slot.shape[1]), 0)
+    out_ref[...] = jnp.sum(jnp.where(here, chosen, 0.0), axis=0, keepdims=True)
+
+
+def take(slot, answer):
+    return pl.pallas_call(
+        take_kernel,
+        out_shape=jax.ShapeDtypeStruct(slot.shape, jnp.float32),
+        in_specs=[VMEM, VMEM],
+        out_specs=VMEM,
+        compiler_params=ROOM,
+    )(slot, answer).reshape(-1)
 
 
 def swap(value, axis):
@@ -83,26 +104,23 @@
     recv = lax.all_to_all(
         send.reshape(peers, 2, width + META), PEERS, split_axis=0, concat_axis=0, tiled=True
     ).reshape(slots, width + META)
+    core, far = lax.axis_index("core"), lax.axis_index("far")
     rows, mark = recv[:, :width], recv[:, width]
-    core, far = lax.axis_index("core"), lax.axis_index("far")
     far_rows, far_mark = swap(rows, "far"), swap(mark, "far")
-    core_rows, core_mark = swap(rows, "core"), swap(mark, "core")
-    both_rows, both_mark = swap(far_rows, "core"), swap(far_mark, "core")
+    core_recv = swap(recv, "core")
+    core_rows, core_mark = core_recv[:, :width], core_recv[:, width]
     mine = (mark, order_of(slots, core, far))
+    twin = (core_mark, order_of(slots, 1 - core, far))
+    beyond = (far_mark, order_of(slots, core, 1 - far))
+    lent = swap(best(core_rows, twin, far_rows, beyond), "core")
     nearest = best(rows, mine, rows, mine)
-    for key, key_mark, c, f in (
-        (core_rows, core_mark, 1 - core, far),
-        (far_rows, far_mark, core, 1 - far),
-        (both_rows, both_mark, 1 - core, 1 - far),
-    ):
-        found = best(rows, mine, key, (key_mark, order_of(slots, c, f)))
-        nearest = jnp.maximum(nearest, found)
+    nearest = jnp.maximum(nearest, best(rows, mine, core_rows, twin))
+    nearest = jnp.maximum(nearest, best(rows, mine, far_rows, beyond))
+    nearest = jnp.maximum(nearest, lent)
     answer = lax.all_to_all(
         nearest.reshape(peers, 1, 2), PEERS, split_axis=0, concat_axis=0, tiled=True
-    ).reshape(peers, 2)
-    chosen = jnp.where((slot & 1) == 0, answer[:, 0:1], answer[:, 1:2])
-    here = (slot >> 1) == lax.broadcasted_iota(jnp.int32, (peers, docs), 0)
-    return jnp.sum(jnp.where(here, chosen, jnp.float32(0.0)), axis=0)
+    )
+    return take(slot, answer.reshape(peers, 2))
 
 
 def solution(mesh):

time: 86.4 us -> 82.2 us (0.951)
  blocking collectives: 0 us -> 57.2 us
  starting transfers between devices: 50.2 us -> 15.8 us
  waiting for transfers between devices: 29 us -> 3.81 us
  local copies, waits for them, and re-layouts: 3.95 us -> 2.45 us
    all_to_all x0 -> x2, blocking collectives: none -> 57.2 us  [the longest x1 37 us: per_device(): lax.all_to_all(send.reshape(peers, 2, width + META), PEERS, split_axis=0,...]
    all_to_all x2 -> x0, starting transfers between devices: 28.9 us -> none  [the longest x1 19.3 us: per_device(): lax.all_to_all(send.reshape(peers, 2, width + META), PEERS, split_axis=0,...]
    all_to_all x2 -> x0, waiting for transfers between devices: 28.7 us -> none  [the longest x1 17.9 us: per_device(): lax.all_to_all(send.reshape(peers, 2, width + META), PEERS, split_axis=0,...]
    ppermute x6 -> x4, starting transfers between devices: 21.4 us -> 15.8 us  [swap(): return lax.ppermute(value, axis, [(0, 1), (1, 0)])]
    ppermute x6 -> x4, waiting for transfers between devices: 0.32 us -> 3.81 us  [swap(): return lax.ppermute(value, axis, [(0, 1), (1, 0)])]
  transfers between devices with their start and end apart: 8 -> 4, of which waited for: 3 -> 2; matrix products, arithmetic and copies ran while one was open for 1% -> 1% of each run, Pallas kernels for 0% -> 0%
where the time goes in v4:
time: 82.2 us; the launch traced here: 81.9 us
  blocking collectives  57.2 us (70%)
  starting transfers between devices  15.8 us (19%)
  waiting for transfers between devices  3.81 us (5%)
  local copies, waits for them, and re-layouts  2.45 us (3%)
  matrix products  1.44 us (2%)
  Pallas kernels  1.05 us (1%)
    all_to_all x1, blocking collectives, per_device(): lax.all_to_all(send.reshape(peers, 2, width + META), PEERS, split_axis=0,...  37 us
    all_to_all x1, blocking collectives, per_device(): lax.all_to_all(nearest.reshape(peers, 1, 2), PEERS, split_axis=0, concat_...  20.2 us
    ppermute x4, starting transfers between devices, swap(): return lax.ppermute(value, axis, [(0, 1), (1, 0)])  15.8 us
    ppermute x4, waiting for transfers between devices, swap(): return lax.ppermute(value, axis, [(0, 1), (1, 0)])  3.81 us
  transfers between devices with their start and end apart: 4, of which 2 were waited for; matrix products, arithmetic and copies ran while one was open for 1% of the time, Pallas kernels for 0%

profile of v4, /device:TPU:1, one launch (start us, length us, event | category | flops | bytes accessed | tf_op | source)
XLA Modules:
  0.0 81.9 jit_solution(1874529779005180152)
XLA Ops:
  0.0 0.0 copy-start.1
  0.0 0.7 copy-done.1
  0.7 0.0 copy-start
  0.7 0.9 %copy-done = bf16[128,1024]{1,0:T(8,128)(2,1)S(1)} copy-done((bf16[128,1024]{1,0:T(8,128)(2,1)S(1)}, bf16[128,1024]{1,0:T(8,128)(2,1)}, u32[]{:S(2)}) %copy-start) | copy-done | bytes 262168
  1.6 0.4 shard_map.28
  2.0 0.2 reshape.155
  2.3 37.0 %all_to_all.10 = bf16[128,2,1152]{2,1,0:T(2,128)(2,1)S(1)} all-to-all(bf16[128,2,1152]{2,1,0:T(2,128)(2,1)S(1)} %reshape.155), channel_id=1, replica_groups=mesh['chip'=64,'core'=2,'far'=2,'near'=2] {'chip','near'}, dimensions={0} | all-to-all | bytes 1179648 | tf_op jit(solution)/shard_map/all_to_all | solution.py:104
  39.3 0.2 reshape.156
  39.5 0.1 slice.17
  39.5 4.4 %collective-permute-start.2 = (bf16[256,1024]{1,0:T(8,128)(2,1)S(1)}, bf16[256,1024]{1,0:T(8,128)(2,1)S(1)}, u32[]{:S(2)}, u32[]{:S(2)}) collective-permute-start(bf16[256,1024]{1,0:T(8,128)(2,1)S(1)} %slice.17), channel_id=1, source_target_pairs={{0,2},{2,0},{1,3},{3,1},{4,6},{6,4},{5,7},{7,5},{8,10},{10,8},{9,1... | collective-permute-start | bytes 1572872 | tf_op jit(solution)/shard_map/ppermute | solution.py:79
  43.9 6.0 %collective-permute-start = (bf16[256,1152]{1,0:T(8,128)(2,1)S(1)}, bf16[256,1152]{1,0:T(8,128)(2,1)S(1)}, u32[]{:S(2)}, u32[]{:S(2)}) collective-permute-start(bf16[256,1152]{1,0:T(8,128)(2,1)S(1)} %reshape.156), channel_id=1, source_target_pairs={{0,4},{4,0},{1,5},{5,1},{2,6},{6,2},{3,7},{7,3},{8,12},{12,8},{9,1... | collective-permute-start | bytes 1769480 | tf_op jit(solution)/shard_map/ppermute | solution.py:79
  50.0 0.1 slice_reduce_fusion.1
  50.1 2.4 %collective-permute-start.1 = (bf16[256]{0:T(256)(128)(2,1)S(1)}, bf16[256]{0:T(256)(128)(2,1)S(1)}, u32[]{:S(2)}, u32[]{:S(2)}) collective-permute-start(bf16[256]{0:T(256)(128)(2,1)S(1)} %slice_reduce_fusion.1), channel_id=1, source_target_pairs={{0,2},{2,0},{1,3},{3,1},{4,6},{6,4},{5,7},{7,5},{8,10},{10,8},{9,1... | collective-permute-start | bytes 1544 | tf_op jit(solution)/shard_map/ppermute | solution.py:79
  52.6 0.4 fusion
  52.9 3.4 %collective-permute-done.1 = bf16[256]{0:T(256)(128)(2,1)S(1)} collective-permute-done((bf16[256]{0:T(256)(128)(2,1)S(1)}, bf16[256]{0:T(256)(128)(2,1)S(1)}, u32[]{:S(2)}, u32[]{:S(2)}) %collective-permute-start.1) | collective-permute-done | bytes 544 | tf_op jit(solution)/shard_map/ppermute | solution.py:79
  56.3 0.0 collective-permute-done.2
  56.3 0.4 select_reduce_fusion.1
  56.7 0.0 collective-permute-done
  56.7 0.1 slice_reduce_fusion
  56.8 0.4 select_reduce_fusion
  57.1 3.0 %collective-permute-start.3 = (f32[256]{0:T(256)S(1)}, f32[256]{0:T(256)S(1)}, u32[]{:S(2)}, u32[]{:S(2)}) collective-permute-start(f32[256]{0:T(256)S(1)} %select_reduce_fusion), channel_id=1, source_target_pairs={{0,4},{4,0},{1,5},{5,1},{2,6},{6,2},{3,7},{7,3},{8,12},{12,8},{9,1... | collective-permute-start | bytes 3080 | tf_op jit(solution)/shard_map/ppermute | solution.py:79
  60.1 0.4 select_reduce_fusion.2
  60.5 0.4 collective-permute-done.3
  60.9 0.1 reshape.157
  61.1 20.2 %all_to_all.11 = f32[128,1,2]{2,1,0:T(1,128)S(1)} all-to-all(f32[128,1,2]{2,1,0:T(1,128)S(1)} %bitcast.8), channel_id=1, replica_groups=mesh['chip'=64,'core'=2,'far'=2,'near'=2] {'chip','near'}, dimensions={0} | all-to-all | bytes 2048 | tf_op jit(solution)/shard_map/all_to_all | solution.py:120
  81.3 0.6 shard_map.29
  (3 shorter events, 0.0 us)
Async XLA Ops:
  0.0 0.7 copy-start.1
  0.7 0.9 %copy-start = (bf16[128,1024]{1,0:T(8,128)(2,1)S(1)}, bf16[128,1024]{1,0:T(8,128)(2,1)}, u32[]{:S(2)}) copy-start(bf16[128,1024]{1,0:T(8,128)(2,1)} %emb_ref.1) | copy-start | bytes 786436
  39.5 16.7 %collective-permute-start.2 = (bf16[256,1024]{1,0:T(8,128)(2,1)S(1)}, bf16[256,1024]{1,0:T(8,128)(2,1)S(1)}, u32[]{:S(2)}, u32[]{:S(2)}) collective-permute-start(bf16[256,1024]{1,0:T(8,128)(2,1)S(1)} %slice.17), channel_id=1, source_target_pairs={{0,2},{2,0},{1,3},{3,1},{4,6},{6,4},{5,7},{7,5},{8,10},{10,8},{9,1... | collective-permute-start | bytes 1572872 | tf_op jit(solution)/shard_map/ppermute | solution.py:79
  43.9 12.7 %collective-permute-start = (bf16[256,1152]{1,0:T(8,128)(2,1)S(1)}, bf16[256,1152]{1,0:T(8,128)(2,1)S(1)}, u32[]{:S(2)}, u32[]{:S(2)}) collective-permute-start(bf16[256,1152]{1,0:T(8,128)(2,1)S(1)} %reshape.156), channel_id=1, source_target_pairs={{0,4},{4,0},{1,5},{5,1},{2,6},{6,2},{3,7},{7,3},{8,12},{12,8},{9,1... | collective-permute-start | bytes 1769480 | tf_op jit(solution)/shard_map/ppermute | solution.py:79
  50.1 6.2 %collective-permute-start.1 = (bf16[256]{0:T(256)(128)(2,1)S(1)}, bf16[256]{0:T(256)(128)(2,1)S(1)}, u32[]{:S(2)}, u32[]{:S(2)}) collective-permute-start(bf16[256]{0:T(256)(128)(2,1)S(1)} %slice_reduce_fusion.1), channel_id=1, source_target_pairs={{0,2},{2,0},{1,3},{3,1},{4,6},{6,4},{5,7},{7,5},{8,10},{10,8},{9,1... | collective-permute-start | bytes 1544 | tf_op jit(solution)/shard_map/ppermute | solution.py:79
  57.1 3.8 %collective-permute-start.3 = (f32[256]{0:T(256)S(1)}, f32[256]{0:T(256)S(1)}, u32[]{:S(2)}, u32[]{:S(2)}) collective-permute-start(f32[256]{0:T(256)S(1)} %select_reduce_fusion), channel_id=1, source_target_pairs={{0,4},{4,0},{1,5},{5,1},{2,6},{6,2},{3,7},{7,3},{8,12},{12,8},{9,1... | collective-permute-start | bytes 3080 | tf_op jit(solution)/shard_map/ppermute | solution.py:79

commit v5 on v4

--- a/solution.py
+++ b/solution.py
@@ -75,25 +75,89 @@
     )(slot, answer).reshape(-1)
 
 
+def found(key, key_mark, key_at, query, query_mark, query_at):
+    scores = lax.dot_general(
+        key, query, (((1,), (1,)), ((), ())), preferred_element_type=jnp.float32
+    )
+
+    def order(axis, at):
+        slot = lax.broadcasted_iota(jnp.int32, scores.shape, axis)
+        return (slot >> 2) * 16 + (slot & 3) + (at[0] * 8 + at[1] * 4)
+
+    allowed = (key_mark == query_mark) & (order(0, key_at) < order(1, query_at))
+    return jnp.max(jnp.where(allowed, scores, -1.0), axis=0, keepdims=True)
+
+
+def column(ref):
+    return ref[:, -META:].astype(jnp.float32)[:, 0:1]
+
+
+HEAD = 16
+
+
+def row_column(ref):
+    row = jnp.broadcast_to(ref[...].astype(jnp.float32), (META, ref.shape[1]))
+    return jnp.transpose(row)[:, 0:1]
+
+
+def lent_kernel(head_ref, beyond_ref, beyond_mark_ref, twin_ref, twin_mark_ref, out_ref):
+    core, far = lax.axis_index("core"), lax.axis_index("far")
+    key = jnp.concatenate([head_ref[...], beyond_ref[HEAD:, :]], axis=0)
+    out_ref[...] = found(
+        key,
+        row_column(beyond_mark_ref),
+        (core, 1 - far),
+        twin_ref[...],
+        twin_mark_ref[...].astype(jnp.float32),
+        (1 - core, far),
+    )
+
+
+def lend(beyond, beyond_mark, twin, twin_mark):
+    slots, width = beyond.shape
+    return pl.pallas_call(
+        lent_kernel,
+        out_shape=jax.ShapeDtypeStruct((1, slots), jnp.float32),
+        in_specs=[VMEM] * 5,
+        out_specs=VMEM,
+        compiler_params=ROOM,
+        cost_estimate=pl.CostEstimate(
+            flops=2 * slots * slots * width, bytes_accessed=4 * slots * width, transcendentals=0
+        ),
+    )(beyond[:HEAD], beyond, beyond_mark.reshape(1, slots), twin, twin_mark.reshape(1, slots))
+
+
+def mine_kernel(
+    recv_ref, twin_ref, beyond_ref, mark_ref, twin_mark_ref, beyond_mark_ref, out_ref
+):
+    core, far = lax.axis_index("core"), lax.axis_index("far")
+    query = recv_ref[:, :-META]
+    mark = mark_ref[...].astype(jnp.float32)
+    at = (core, far)
+    best = found(query, column(recv_ref), at, query, mark, at)
+    twin = found(twin_ref[...], row_column(twin_mark_ref), (1 - core, far), query, mark, at)
+    beyond = found(
+        beyond_ref[...], row_column(beyond_mark_ref), (core, 1 - far), query, mark, at
+    )
+    out_ref[...] = jnp.maximum(best, jnp.maximum(twin, beyond))
+
+
+def best_of_mine(recv, twin, beyond, *marks):
+    slots, width = beyond.shape
+    return pl.pallas_call(
+        mine_kernel,
+        out_shape=jax.ShapeDtypeStruct((1, slots), jnp.float32),
+        in_specs=[VMEM] * 6,
+        out_specs=VMEM,
+        compiler_params=ROOM,
+        cost_estimate=pl.CostEstimate(
+            flops=6 * slots * slots * width, bytes_accessed=6 * slots * width, transcendentals=0
+        ),
+    )(recv, twin, beyond, *(m.reshape(1, slots) for m in marks))
+
+
 def swap(value, axis):
     return lax.ppermute(value, axis, [(0, 1), (1, 0)])
-
-
-def order_of(count, core, far):
-    slot = lax.iota(jnp.int32, count)
-    peer, rank = slot // 2, slot % 2
-    device = (((peer // 2) * 2 + core) * 2 + far) * 2 + peer % 2
-    return device * 2 + rank
-
-
-def best(query, query_meta, key, key_meta):
-    scores = lax.dot_general(
-        query, key, (((1,), (1,)), ((), ())), preferred_element_type=jnp.float32
-    )
-    allowed = (query_meta[0][:, None] == key_meta[0][None, :]) & (
-        key_meta[1][None, :] < query_meta[1][:, None]
-    )
-    return jnp.max(jnp.where(allowed, scores, jnp.float32(-1.0)), axis=1)
 
 
 def per_device(embeddings, cluster_ids):
@@ -104,19 +168,11 @@
     recv = lax.all_to_all(
         send.reshape(peers, 2, width + META), PEERS, split_axis=0, concat_axis=0, tiled=True
     ).reshape(slots, width + META)
-    core, far = lax.axis_index("core"), lax.axis_index("far")
     rows, mark = recv[:, :width], recv[:, width]
     far_rows, far_mark = swap(rows, "far"), swap(mark, "far")
-    core_recv = swap(recv, "core")
-    core_rows, core_mark = core_recv[:, :width], core_recv[:, width]
-    mine = (mark, order_of(slots, core, far))
-    twin = (core_mark, order_of(slots, 1 - core, far))
-    beyond = (far_mark, order_of(slots, core, 1 - far))
-    lent = swap(best(core_rows, twin, far_rows, beyond), "core")
-    nearest = best(rows, mine, rows, mine)
-    nearest = jnp.maximum(nearest, best(rows, mine, core_rows, twin))
-    nearest = jnp.maximum(nearest, best(rows, mine, far_rows, beyond))
-    nearest = jnp.maximum(nearest, lent)
+    twin, twin_mark = swap(rows, "core"), swap(mark, "core")
+    lent = swap(lend(far_rows, far_mark, twin, twin_mark), "core")
+    nearest = jnp.maximum(best_of_mine(recv, twin, far_rows, mark, twin_mark, far_mark), lent)
     answer = lax.all_to_all(
         nearest.reshape(peers, 1, 2), PEERS, split_axis=0, concat_axis=0, tiled=True
     )

time: 82.2 us -> 81.8 us (level)
  starting transfers between devices: 15.8 us -> 18.3 us
  blocking collectives: 57.2 us -> 55.1 us
  matrix products: 1.44 us -> 0 us
  Pallas kernels: 1.05 us -> 2.05 us
    ppermute x4 -> x5, starting transfers between devices: 15.8 us -> 18.3 us  [swap(): return lax.ppermute(value, axis, [(0, 1), (1, 0)])]
    all_to_all x1, blocking collectives: 20.2 us -> 18.1 us  [per_device(): lax.all_to_all(nearest.reshape(peers, 1, 2), PEERS, split_axis=0, concat_...]
    dot_general x4 -> x0, matrix products: 1.44 us -> none  [best(): lax.dot_general(query, key, (((1,), (1,)), ((), ())), preferred_element_t...]
    pallas_call x0 -> x2, Pallas kernels: none -> 1 us  [the longest x1 0.65 us: best_of_mine(): pl.pallas_call(mine_kernel, out_shape=jax.ShapeDtypeStruct((1, slots), jn...]
    ppermute x4 -> x5, waiting for transfers between devices: 3.81 us -> 3.48 us  [swap(): return lax.ppermute(value, axis, [(0, 1), (1, 0)])]
  transfers between devices with their start and end apart: 4 -> 5, of which waited for: 2 -> 2; matrix products, arithmetic and copies ran while one was open for 1% -> 0% of each run, Pallas kernels for 0% -> 1%
where the time goes in v5:
time: 81.8 us; the launch traced here: 81.5 us
  blocking collectives  55.1 us (67%)
  starting transfers between devices  18.3 us (22%)
  waiting for transfers between devices  3.48 us (4%)
  local copies, waits for them, and re-layouts  2.36 us (3%)
  Pallas kernels  2.05 us (3%)
    all_to_all x1, blocking collectives, per_device(): lax.all_to_all(send.reshape(peers, 2, width + META), PEERS, split_axis=0,...  37 us
    ppermute x5, starting transfers between devices, swap(): return lax.ppermute(value, axis, [(0, 1), (1, 0)])  18.3 us
    all_to_all x1, blocking collectives, per_device(): lax.all_to_all(nearest.reshape(peers, 1, 2), PEERS, split_axis=0, concat_...  18.1 us
    ppermute x5, waiting for transfers between devices, swap(): return lax.ppermute(value, axis, [(0, 1), (1, 0)])  3.48 us
  transfers between devices with their start and end apart: 5, of which 2 were waited for; matrix products, arithmetic and copies ran while one was open for 0% of the time, Pallas kernels for 1%

profile of v5, /device:TPU:1, one launch (start us, length us, event | category | flops | bytes accessed | tf_op | source)
XLA Modules:
  0.0 81.5 jit_solution(6117065308704327180)
XLA Ops:
  0.0 0.0 copy-start.1
  0.0 0.7 copy-done.1
  0.7 0.0 copy-start
  0.7 0.9 %copy-done = bf16[128,1024]{1,0:T(8,128)(2,1)S(1)} copy-done((bf16[128,1024]{1,0:T(8,128)(2,1)S(1)}, bf16[128,1024]{1,0:T(8,128)(2,1)}, u32[]{:S(2)}) %copy-start) | copy-done | bytes 262168
  1.6 0.4 shard_map.28
  2.0 0.2 reshape.27
  2.3 37.0 %all_to_all.10 = bf16[128,2,1152]{2,1,0:T(2,128)(2,1)S(1)} all-to-all(bf16[128,2,1152]{2,1,0:T(2,128)(2,1)S(1)} %reshape.27), channel_id=1, replica_groups=mesh['chip'=64,'core'=2,'far'=2,'near'=2] {'chip','near'}, dimensions={0} | all-to-all | bytes 1179648 | tf_op jit(solution)/shard_map/all_to_all | solution.py:168
  39.3 0.2 reshape.28.recv_ref
  39.5 0.1 slice.12
  39.5 4.4 %collective-permute-start.1 = (bf16[256,1024]{1,0:T(8,128)(2,1)S(1)}, bf16[256,1024]{1,0:T(8,128)(2,1)S(1)}, u32[]{:S(2)}, u32[]{:S(2)}) collective-permute-start(bf16[256,1024]{1,0:T(8,128)(2,1)S(1)} %slice.12), channel_id=1, source_target_pairs={{0,2},{2,0},{1,3},{3,1},{4,6},{6,4},{5,7},{7,5},{8,10},{10,8},{9,1... | collective-permute-start | bytes 1572872 | tf_op jit(solution)/shard_map/ppermute | solution.py:160
  43.9 6.0 %collective-permute-start = (bf16[256,1024]{1,0:T(8,128)(2,1)S(1)}, bf16[256,1024]{1,0:T(8,128)(2,1)S(1)}, u32[]{:S(2)}, u32[]{:S(2)}) collective-permute-start(bf16[256,1024]{1,0:T(8,128)(2,1)S(1)} %slice.12), channel_id=1, source_target_pairs={{0,4},{4,0},{1,5},{5,1},{2,6},{6,2},{3,7},{7,3},{8,12},{12,8},{9,1... | collective-permute-start | bytes 1572872 | tf_op jit(solution)/shard_map/ppermute | solution.py:160
  50.0 0.1 slice_reduce_fusion
  50.1 1.9 %collective-permute-start.2 = (bf16[256]{0:T(256)(128)(2,1)S(1)}, bf16[256]{0:T(256)(128)(2,1)S(1)}, u32[]{:S(2)}, u32[]{:S(2)}) collective-permute-start(bf16[256]{0:T(256)(128)(2,1)S(1)} %slice_reduce_fusion), channel_id=1, source_target_pairs={{0,4},{4,0},{1,5},{5,1},{2,6},{6,2},{3,7},{7,3},{8,12},{12,8},{9,1... | collective-permute-start | bytes 1544 | tf_op jit(solution)/shard_map/ppermute | solution.py:160
  52.0 2.4 %collective-permute-start.3 = (bf16[256]{0:T(256)(128)(2,1)S(1)}, bf16[256]{0:T(256)(128)(2,1)S(1)}, u32[]{:S(2)}, u32[]{:S(2)}) collective-permute-start(bf16[256]{0:T(256)(128)(2,1)S(1)} %slice_reduce_fusion), channel_id=1, source_target_pairs={{0,2},{2,0},{1,3},{3,1},{4,6},{6,4},{5,7},{7,5},{8,10},{10,8},{9,1... | collective-permute-start | bytes 1544 | tf_op jit(solution)/shard_map/ppermute | solution.py:160
  54.5 0.0 collective-permute-done.2
  54.5 3.3 %collective-permute-done.3 = bf16[256]{0:T(256)(128)(2,1)S(1)} collective-permute-done((bf16[256]{0:T(256)(128)(2,1)S(1)}, bf16[256]{0:T(256)(128)(2,1)S(1)}, u32[]{:S(2)}, u32[]{:S(2)}) %collective-permute-start.3) | collective-permute-done | bytes 544 | tf_op jit(solution)/shard_map/ppermute | solution.py:160
  57.8 0.0 collective-permute-done.1.beyond_ref
  57.8 0.0 collective-permute-done.twin_ref
  57.8 0.4 shard_map.30
  58.2 3.6 %collective-permute-start.4 = (f32[1,256]{1,0:T(1,128)S(1)}, f32[1,256]{1,0:T(1,128)S(1)}, u32[]{:S(2)}, u32[]{:S(2)}) collective-permute-start(f32[1,256]{1,0:T(1,128)S(1)} %shard_map.30), channel_id=1, source_target_pairs={{0,4},{4,0},{1,5},{5,1},{2,6},{6,2},{3,7},{7,3},{8,12},{12,8},{9,1... | collective-permute-start | bytes 3080 | tf_op jit(solution)/shard_map/ppermute | solution.py:160
  61.7 0.6 shard_map.29
  62.4 0.1 collective-permute-done.4
  62.6 0.1 reshape.31
  62.7 18.1 %all_to_all.11 = f32[128,1,2]{2,1,0:T(1,128)S(1)} all-to-all(f32[128,1,2]{2,1,0:T(1,128)S(1)} %bitcast.6), channel_id=1, replica_groups=mesh['chip'=64,'core'=2,'far'=2,'near'=2] {'chip','near'}, dimensions={0} | all-to-all | bytes 2048 | tf_op jit(solution)/shard_map/all_to_all | solution.py:176
  80.8 0.6 shard_map.31
  (5 shorter events, 0.0 us)
Async XLA Ops:
  0.0 0.7 copy-start.1
  0.7 0.9 %copy-start = (bf16[128,1024]{1,0:T(8,128)(2,1)S(1)}, bf16[128,1024]{1,0:T(8,128)(2,1)}, u32[]{:S(2)}) copy-start(bf16[128,1024]{1,0:T(8,128)(2,1)} %emb_ref.1) | copy-start | bytes 786436
  39.5 18.3 %collective-permute-start.1 = (bf16[256,1024]{1,0:T(8,128)(2,1)S(1)}, bf16[256,1024]{1,0:T(8,128)(2,1)S(1)}, u32[]{:S(2)}, u32[]{:S(2)}) collective-permute-start(bf16[256,1024]{1,0:T(8,128)(2,1)S(1)} %slice.12), channel_id=1, source_target_pairs={{0,2},{2,0},{1,3},{3,1},{4,6},{6,4},{5,7},{7,5},{8,10},{10,8},{9,1... | collective-permute-start | bytes 1572872 | tf_op jit(solution)/shard_map/ppermute | solution.py:160
  43.9 13.9 %collective-permute-start = (bf16[256,1024]{1,0:T(8,128)(2,1)S(1)}, bf16[256,1024]{1,0:T(8,128)(2,1)S(1)}, u32[]{:S(2)}, u32[]{:S(2)}) collective-permute-start(bf16[256,1024]{1,0:T(8,128)(2,1)S(1)} %slice.12), channel_id=1, source_target_pairs={{0,4},{4,0},{1,5},{5,1},{2,6},{6,2},{3,7},{7,3},{8,12},{12,8},{9,1... | collective-permute-start | bytes 1572872 | tf_op jit(solution)/shard_map/ppermute | solution.py:160
  50.1 4.4 %collective-permute-start.2 = (bf16[256]{0:T(256)(128)(2,1)S(1)}, bf16[256]{0:T(256)(128)(2,1)S(1)}, u32[]{:S(2)}, u32[]{:S(2)}) collective-permute-start(bf16[256]{0:T(256)(128)(2,1)S(1)} %slice_reduce_fusion), channel_id=1, source_target_pairs={{0,4},{4,0},{1,5},{5,1},{2,6},{6,2},{3,7},{7,3},{8,12},{12,8},{9,1... | collective-permute-start | bytes 1544 | tf_op jit(solution)/shard_map/ppermute | solution.py:160
  52.0 5.8 %collective-permute-start.3 = (bf16[256]{0:T(256)(128)(2,1)S(1)}, bf16[256]{0:T(256)(128)(2,1)S(1)}, u32[]{:S(2)}, u32[]{:S(2)}) collective-permute-start(bf16[256]{0:T(256)(128)(2,1)S(1)} %slice_reduce_fusion), channel_id=1, source_target_pairs={{0,2},{2,0},{1,3},{3,1},{4,6},{6,4},{5,7},{7,5},{8,10},{10,8},{9,1... | collective-permute-start | bytes 1544 | tf_op jit(solution)/shard_map/ppermute | solution.py:160
  58.2 4.4 %collective-permute-start.4 = (f32[1,256]{1,0:T(1,128)S(1)}, f32[1,256]{1,0:T(1,128)S(1)}, u32[]{:S(2)}, u32[]{:S(2)}) collective-permute-start(f32[1,256]{1,0:T(1,128)S(1)} %shard_map.30), channel_id=1, source_target_pairs={{0,4},{4,0},{1,5},{5,1},{2,6},{6,2},{3,7},{7,3},{8,12},{12,8},{9,1... | collective-permute-start | bytes 3080 | tf_op jit(solution)/shard_map/ppermute | solution.py:160

commit v6 on v5

--- a/solution.py
+++ b/solution.py
@@ -21,7 +21,7 @@
     owner = (ids * 43691) >> 21
     label = (ids - owner * CL_DEV + 1).astype(jnp.float32)
     slot = lax.broadcasted_iota(jnp.int32, (slots, docs), 0)
-    mine = (slot >> 1) == owner
+    mine = (slot >> 1) == (owner ^ lax.axis_index("far"))
     square = (docs, docs)
     earlier = lax.broadcasted_iota(jnp.int32, square, 0) < lax.broadcasted_iota(
         jnp.int32, square, 1
@@ -160,6 +160,10 @@
     return lax.ppermute(value, axis, [(0, 1), (1, 0)])
 
 
+def cross(value):
+    return lax.ppermute(value, ("far", "near"), [(x, 3 - x) for x in range(4)])
+
+
 def per_device(embeddings, cluster_ids):
     docs, width = embeddings.shape
     peers = lax.axis_size("chip") * lax.axis_size("near")
@@ -169,7 +173,7 @@
         send.reshape(peers, 2, width + META), PEERS, split_axis=0, concat_axis=0, tiled=True
     ).reshape(slots, width + META)
     rows, mark = recv[:, :width], recv[:, width]
-    far_rows, far_mark = swap(rows, "far"), swap(mark, "far")
+    far_rows, far_mark = cross(rows), cross(mark)
     twin, twin_mark = swap(rows, "core"), swap(mark, "core")
     lent = swap(lend(far_rows, far_mark, twin, twin_mark), "core")
     nearest = jnp.maximum(best_of_mine(recv, twin, far_rows, mark, twin_mark, far_mark), lent)

time: 81.8 us -> 81.5 us (level); the launches traced: 81.5 us -> 80.3 us
    ppermute x5 -> x3, starting transfers between devices: 18.3 us -> 10.6 us  [swap(): return lax.ppermute(value, axis, [(0, 1), (1, 0)])]
    ppermute x0 -> x2, starting transfers between devices: none -> 7.36 us  [cross(): return lax.ppermute(value, ('far', 'near'), [(x, 3 - x) for x in range(4)])]
    ppermute x0 -> x2, waiting for transfers between devices: none -> 3.36 us  [cross(): return lax.ppermute(value, ('far', 'near'), [(x, 3 - x) for x in range(4)])]
    ppermute x5 -> x3, waiting for transfers between devices: 3.48 us -> 0.15 us  [swap(): return lax.ppermute(value, axis, [(0, 1), (1, 0)])]
    all_to_all x1, blocking collectives: 18.1 us -> 17.3 us  [per_device(): lax.all_to_all(nearest.reshape(peers, 1, 2), PEERS, split_axis=0, concat_...]
where the time goes in v6:
time: 81.5 us; the launch traced here: 80.3 us
  blocking collectives  54.3 us (67%)
  starting transfers between devices  18 us (22%)
  waiting for transfers between devices  3.51 us (4%)
  local copies, waits for them, and re-layouts  2.36 us (3%)
  Pallas kernels  2.04 us (3%)
    all_to_all x1, blocking collectives, per_device(): lax.all_to_all(send.reshape(peers, 2, width + META), PEERS, split_axis=0,...  37 us
    all_to_all x1, blocking collectives, per_device(): lax.all_to_all(nearest.reshape(peers, 1, 2), PEERS, split_axis=0, concat_...  17.3 us
    ppermute x3, starting transfers between devices, swap(): return lax.ppermute(value, axis, [(0, 1), (1, 0)])  10.6 us
    ppermute x2, starting transfers between devices, cross(): return lax.ppermute(value, ('far', 'near'), [(x, 3 - x) for x in range(4)])  7.36 us
    ppermute x2, waiting for transfers between devices, cross(): return lax.ppermute(value, ('far', 'near'), [(x, 3 - x) for x in range(4)])  3.36 us
  transfers between devices with their start and end apart: 5, of which 2 were waited for; matrix products, arithmetic and copies ran while one was open for 0% of the time, Pallas kernels for 1%

profile of v6, /device:TPU:1, one launch (start us, length us, event | category | flops | bytes accessed | tf_op | source)
XLA Modules:
  0.0 80.3 jit_solution(8399713582709250324)
XLA Ops:
  0.0 0.0 copy-start.1
  0.0 0.7 copy-done.1
  0.7 0.0 copy-start
  0.7 0.9 %copy-done = bf16[128,1024]{1,0:T(8,128)(2,1)S(1)} copy-done((bf16[128,1024]{1,0:T(8,128)(2,1)S(1)}, bf16[128,1024]{1,0:T(8,128)(2,1)}, u32[]{:S(2)}) %copy-start) | copy-done | bytes 262168
  1.6 0.4 shard_map.28
  2.0 0.2 reshape.27
  2.3 37.0 %all_to_all.10 = bf16[128,2,1152]{2,1,0:T(2,128)(2,1)S(1)} all-to-all(bf16[128,2,1152]{2,1,0:T(2,128)(2,1)S(1)} %reshape.27), channel_id=1, replica_groups=mesh['chip'=64,'core'=2,'far'=2,'near'=2] {'chip','near'}, dimensions={0} | all-to-all | bytes 1179648 | tf_op jit(solution)/shard_map/all_to_all | solution.py:172
  39.3 0.2 reshape.28.recv_ref
  39.5 0.1 slice.12
  39.5 5.3 %collective-permute-start.1 = (bf16[256,1024]{1,0:T(8,128)(2,1)S(1)}, bf16[256,1024]{1,0:T(8,128)(2,1)S(1)}, u32[]{:S(2)}, u32[]{:S(2)}) collective-permute-start(bf16[256,1024]{1,0:T(8,128)(2,1)S(1)} %slice.12), channel_id=1, source_target_pairs={{0,3},{1,2},{2,1},{3,0},{4,7},{5,6},{6,5},{7,4},{8,11},{9,10},{10,... | collective-permute-start | bytes 1572872 | tf_op jit(solution)/shard_map/ppermute | solution.py:164
  44.8 5.2 %collective-permute-start = (bf16[256,1024]{1,0:T(8,128)(2,1)S(1)}, bf16[256,1024]{1,0:T(8,128)(2,1)S(1)}, u32[]{:S(2)}, u32[]{:S(2)}) collective-permute-start(bf16[256,1024]{1,0:T(8,128)(2,1)S(1)} %slice.12), channel_id=1, source_target_pairs={{0,4},{4,0},{1,5},{5,1},{2,6},{6,2},{3,7},{7,3},{8,12},{12,8},{9,1... | collective-permute-start | bytes 1572872 | tf_op jit(solution)/shard_map/ppermute | solution.py:160
  50.0 0.1 slice_reduce_fusion
  50.1 1.9 %collective-permute-start.2 = (bf16[256]{0:T(256)(128)(2,1)S(1)}, bf16[256]{0:T(256)(128)(2,1)S(1)}, u32[]{:S(2)}, u32[]{:S(2)}) collective-permute-start(bf16[256]{0:T(256)(128)(2,1)S(1)} %slice_reduce_fusion), channel_id=1, source_target_pairs={{0,4},{4,0},{1,5},{5,1},{2,6},{6,2},{3,7},{7,3},{8,12},{12,8},{9,1... | collective-permute-start | bytes 1544 | tf_op jit(solution)/shard_map/ppermute | solution.py:160
  52.0 2.1 %collective-permute-start.3 = (bf16[256]{0:T(256)(128)(2,1)S(1)}, bf16[256]{0:T(256)(128)(2,1)S(1)}, u32[]{:S(2)}, u32[]{:S(2)}) collective-permute-start(bf16[256]{0:T(256)(128)(2,1)S(1)} %slice_reduce_fusion), channel_id=1, source_target_pairs={{0,3},{1,2},{2,1},{3,0},{4,7},{5,6},{6,5},{7,4},{8,11},{9,10},{10,... | collective-permute-start | bytes 1544 | tf_op jit(solution)/shard_map/ppermute | solution.py:164
  54.2 0.0 collective-permute-done.2
  54.2 3.4 %collective-permute-done.3 = bf16[256]{0:T(256)(128)(2,1)S(1)} collective-permute-done((bf16[256]{0:T(256)(128)(2,1)S(1)}, bf16[256]{0:T(256)(128)(2,1)S(1)}, u32[]{:S(2)}, u32[]{:S(2)}) %collective-permute-start.3) | collective-permute-done | bytes 544 | tf_op jit(solution)/shard_map/ppermute | solution.py:164
  57.5 0.0 collective-permute-done.1.beyond_ref
  57.5 0.0 collective-permute-done.twin_ref
  57.6 0.4 shard_map.30
  57.9 3.6 %collective-permute-start.4 = (f32[1,256]{1,0:T(1,128)S(1)}, f32[1,256]{1,0:T(1,128)S(1)}, u32[]{:S(2)}, u32[]{:S(2)}) collective-permute-start(f32[1,256]{1,0:T(1,128)S(1)} %shard_map.30), channel_id=1, source_target_pairs={{0,4},{4,0},{1,5},{5,1},{2,6},{6,2},{3,7},{7,3},{8,12},{12,8},{9,1... | collective-permute-start | bytes 3080 | tf_op jit(solution)/shard_map/ppermute | solution.py:160
  61.5 0.6 shard_map.29
  62.1 0.1 collective-permute-done.4
  62.3 0.1 reshape.31
  62.4 17.3 %all_to_all.11 = f32[128,1,2]{2,1,0:T(1,128)S(1)} all-to-all(f32[128,1,2]{2,1,0:T(1,128)S(1)} %bitcast.6), channel_id=1, replica_groups=mesh['chip'=64,'core'=2,'far'=2,'near'=2] {'chip','near'}, dimensions={0} | all-to-all | bytes 2048 | tf_op jit(solution)/shard_map/all_to_all | solution.py:180
  79.7 0.6 shard_map.31
  (5 shorter events, 0.0 us)
Async XLA Ops:
  0.0 0.7 copy-start.1
  0.7 0.9 %copy-start = (bf16[128,1024]{1,0:T(8,128)(2,1)S(1)}, bf16[128,1024]{1,0:T(8,128)(2,1)}, u32[]{:S(2)}) copy-start(bf16[128,1024]{1,0:T(8,128)(2,1)} %emb_ref.1) | copy-start | bytes 786436
  39.5 18.0 %collective-permute-start.1 = (bf16[256,1024]{1,0:T(8,128)(2,1)S(1)}, bf16[256,1024]{1,0:T(8,128)(2,1)S(1)}, u32[]{:S(2)}, u32[]{:S(2)}) collective-permute-start(bf16[256,1024]{1,0:T(8,128)(2,1)S(1)} %slice.12), channel_id=1, source_target_pairs={{0,3},{1,2},{2,1},{3,0},{4,7},{5,6},{6,5},{7,4},{8,11},{9,10},{10,... | collective-permute-start | bytes 1572872 | tf_op jit(solution)/shard_map/ppermute | solution.py:164
  44.8 12.7 %collective-permute-start = (bf16[256,1024]{1,0:T(8,128)(2,1)S(1)}, bf16[256,1024]{1,0:T(8,128)(2,1)S(1)}, u32[]{:S(2)}, u32[]{:S(2)}) collective-permute-start(bf16[256,1024]{1,0:T(8,128)(2,1)S(1)} %slice.12), channel_id=1, source_target_pairs={{0,4},{4,0},{1,5},{5,1},{2,6},{6,2},{3,7},{7,3},{8,12},{12,8},{9,1... | collective-permute-start | bytes 1572872 | tf_op jit(solution)/shard_map/ppermute | solution.py:160
  50.1 4.0 %collective-permute-start.2 = (bf16[256]{0:T(256)(128)(2,1)S(1)}, bf16[256]{0:T(256)(128)(2,1)S(1)}, u32[]{:S(2)}, u32[]{:S(2)}) collective-permute-start(bf16[256]{0:T(256)(128)(2,1)S(1)} %slice_reduce_fusion), channel_id=1, source_target_pairs={{0,4},{4,0},{1,5},{5,1},{2,6},{6,2},{3,7},{7,3},{8,12},{12,8},{9,1... | collective-permute-start | bytes 1544 | tf_op jit(solution)/shard_map/ppermute | solution.py:160
  52.0 5.5 %collective-permute-start.3 = (bf16[256]{0:T(256)(128)(2,1)S(1)}, bf16[256]{0:T(256)(128)(2,1)S(1)}, u32[]{:S(2)}, u32[]{:S(2)}) collective-permute-start(bf16[256]{0:T(256)(128)(2,1)S(1)} %slice_reduce_fusion), channel_id=1, source_target_pairs={{0,3},{1,2},{2,1},{3,0},{4,7},{5,6},{6,5},{7,4},{8,11},{9,10},{10,... | collective-permute-start | bytes 1544 | tf_op jit(solution)/shard_map/ppermute | solution.py:164
  57.9 4.4 %collective-permute-start.4 = (f32[1,256]{1,0:T(1,128)S(1)}, f32[1,256]{1,0:T(1,128)S(1)}, u32[]{:S(2)}, u32[]{:S(2)}) collective-permute-start(f32[1,256]{1,0:T(1,128)S(1)} %shard_map.30), channel_id=1, source_target_pairs={{0,4},{4,0},{1,5},{5,1},{2,6},{6,2},{3,7},{7,3},{8,12},{12,8},{9,1... | collective-permute-start | bytes 3080 | tf_op jit(solution)/shard_map/ppermute | solution.py:160

commit v7 on v6

--- a/solution.py
+++ b/solution.py
@@ -16,7 +16,8 @@
 
 def place_kernel(ids_ref, emb_ref, out_ref, slot_ref):
     docs, width = emb_ref.shape
-    slots = out_ref.shape[0]
+    peers = out_ref.shape[0]
+    slots = 2 * peers
     ids = ids_ref[...]
     owner = (ids * 43691) >> 21
     label = (ids - owner * CL_DEV + 1).astype(jnp.float32)
@@ -34,11 +35,11 @@
     unit = (
         values * lax.rsqrt(jnp.sum(values * values, axis=1, keepdims=True) + EPSILON)
     ).astype(jnp.bfloat16)
-    out_ref[:, :width] = jnp.dot(
-        pick.astype(jnp.bfloat16), unit, preferred_element_type=jnp.float32
-    ).astype(jnp.bfloat16)
+    rows = jnp.dot(pick.astype(jnp.bfloat16), unit, preferred_element_type=jnp.float32)
+    out_ref[:, :, :width] = rows.astype(jnp.bfloat16).reshape(peers, 2, width)
     mark = jnp.sum(jnp.where(pick, label, 0.0), axis=1, keepdims=True)
-    out_ref[:, width:] = jnp.broadcast_to(mark, (slots, META)).astype(jnp.bfloat16)
+    marks = jnp.broadcast_to(mark, (slots, META)).astype(jnp.bfloat16)
+    out_ref[:, :, width:] = marks.reshape(peers, 2, META)
     slot_ref[...] = jnp.sum(jnp.where(pick, slot, 0), axis=0, keepdims=True)
 
 
@@ -47,7 +48,7 @@
     return pl.pallas_call(
         place_kernel,
         out_shape=(
-            jax.ShapeDtypeStruct((slots, width + META), jnp.bfloat16),
+            jax.ShapeDtypeStruct((slots // 2, 2, width + META), jnp.bfloat16),
             jax.ShapeDtypeStruct((1, docs), jnp.int32),
         ),
         in_specs=[VMEM, VMEM],
@@ -170,7 +171,7 @@
     slots = 2 * peers
     send, slot = place(embeddings, cluster_ids, slots)
     recv = lax.all_to_all(
-        send.reshape(peers, 2, width + META), PEERS, split_axis=0, concat_axis=0, tiled=True
+        send, PEERS, split_axis=0, concat_axis=0, tiled=True
     ).reshape(slots, width + META)
     rows, mark = recv[:, :width], recv[:, width]
     far_rows, far_mark = cross(rows), cross(mark)

time: 81.5 us -> 81.2 us (level)
  no operation moved by 1% of the time
where the time goes in v7:
time: 81.2 us; the launch traced here: 80.1 us
  blocking collectives  54.3 us (67%)
  starting transfers between devices  18 us (22%)
  waiting for transfers between devices  3.5 us (4%)
  local copies, waits for them, and re-layouts  2.14 us (3%)
  Pallas kernels  2.06 us (3%)
    all_to_all x1, blocking collectives, per_device(): lax.all_to_all(send, PEERS, split_axis=0, concat_axis=0, tiled=True)  37 us
    all_to_all x1, blocking collectives, per_device(): lax.all_to_all(nearest.reshape(peers, 1, 2), PEERS, split_axis=0, concat_...  17.3 us
    ppermute x3, starting transfers between devices, swap(): return lax.ppermute(value, axis, [(0, 1), (1, 0)])  10.7 us
    ppermute x2, starting transfers between devices, cross(): return lax.ppermute(value, ('far', 'near'), [(x, 3 - x) for x in range(4)])  7.35 us
    ppermute x2, waiting for transfers between devices, cross(): return lax.ppermute(value, ('far', 'near'), [(x, 3 - x) for x in range(4)])  3.36 us
  transfers between devices with their start and end apart: 5, of which 2 were waited for; matrix products, arithmetic and copies ran while one was open for 0% of the time, Pallas kernels for 1%

profile of v7, /device:TPU:1, one launch (start us, length us, event | category | flops | bytes accessed | tf_op | source)
XLA Modules:
  0.0 80.1 jit_solution(15956753548807032641)
XLA Ops:
  0.0 0.0 copy-start.1
  0.0 0.7 copy-done.1
  0.7 0.0 copy-start
  0.7 0.9 %copy-done = bf16[128,1024]{1,0:T(8,128)(2,1)S(1)} copy-done((bf16[128,1024]{1,0:T(8,128)(2,1)S(1)}, bf16[128,1024]{1,0:T(8,128)(2,1)}, u32[]{:S(2)}) %copy-start) | copy-done | bytes 262168
  1.6 0.4 shard_map.28
  2.1 37.0 %all_to_all.10 = bf16[128,2,1152]{2,1,0:T(2,128)(2,1)S(1)} all-to-all(bf16[128,2,1152]{2,1,0:T(2,128)(2,1)S(1)} %get-tuple-element.8), channel_id=1, replica_groups=mesh['chip'=64,'core'=2,'far'=2,'near'=2] {'chip','near'}, dimensions={0} | all-to-all | bytes 1179648 | tf_op jit(solution)/shard_map/all_to_all | solution.py:173
  39.0 0.2 reshape.24.recv_ref
  39.3 0.1 slice.12
  39.3 5.2 %collective-permute-start.1 = (bf16[256,1024]{1,0:T(8,128)(2,1)S(1)}, bf16[256,1024]{1,0:T(8,128)(2,1)S(1)}, u32[]{:S(2)}, u32[]{:S(2)}) collective-permute-start(bf16[256,1024]{1,0:T(8,128)(2,1)S(1)} %slice.12), channel_id=1, source_target_pairs={{0,3},{1,2},{2,1},{3,0},{4,7},{5,6},{6,5},{7,4},{8,11},{9,10},{10,... | collective-permute-start | bytes 1572872 | tf_op jit(solution)/shard_map/ppermute | solution.py:165
  44.6 5.2 %collective-permute-start = (bf16[256,1024]{1,0:T(8,128)(2,1)S(1)}, bf16[256,1024]{1,0:T(8,128)(2,1)S(1)}, u32[]{:S(2)}, u32[]{:S(2)}) collective-permute-start(bf16[256,1024]{1,0:T(8,128)(2,1)S(1)} %slice.12), channel_id=1, source_target_pairs={{0,4},{4,0},{1,5},{5,1},{2,6},{6,2},{3,7},{7,3},{8,12},{12,8},{9,1... | collective-permute-start | bytes 1572872 | tf_op jit(solution)/shard_map/ppermute | solution.py:161
  49.8 0.1 slice_reduce_fusion
  49.9 1.9 %collective-permute-start.2 = (bf16[256]{0:T(256)(128)(2,1)S(1)}, bf16[256]{0:T(256)(128)(2,1)S(1)}, u32[]{:S(2)}, u32[]{:S(2)}) collective-permute-start(bf16[256]{0:T(256)(128)(2,1)S(1)} %slice_reduce_fusion), channel_id=1, source_target_pairs={{0,4},{4,0},{1,5},{5,1},{2,6},{6,2},{3,7},{7,3},{8,12},{12,8},{9,1... | collective-permute-start | bytes 1544 | tf_op jit(solution)/shard_map/ppermute | solution.py:161
  51.8 2.1 %collective-permute-start.3 = (bf16[256]{0:T(256)(128)(2,1)S(1)}, bf16[256]{0:T(256)(128)(2,1)S(1)}, u32[]{:S(2)}, u32[]{:S(2)}) collective-permute-start(bf16[256]{0:T(256)(128)(2,1)S(1)} %slice_reduce_fusion), channel_id=1, source_target_pairs={{0,3},{1,2},{2,1},{3,0},{4,7},{5,6},{6,5},{7,4},{8,11},{9,10},{10,... | collective-permute-start | bytes 1544 | tf_op jit(solution)/shard_map/ppermute | solution.py:165
  53.9 0.0 collective-permute-done.2
  54.0 3.4 %collective-permute-done.3 = bf16[256]{0:T(256)(128)(2,1)S(1)} collective-permute-done((bf16[256]{0:T(256)(128)(2,1)S(1)}, bf16[256]{0:T(256)(128)(2,1)S(1)}, u32[]{:S(2)}, u32[]{:S(2)}) %collective-permute-start.3) | collective-permute-done | bytes 544 | tf_op jit(solution)/shard_map/ppermute | solution.py:165
  57.3 0.0 collective-permute-done.1.beyond_ref
  57.3 0.0 collective-permute-done.twin_ref
  57.3 0.4 shard_map.30
  57.7 3.6 %collective-permute-start.4 = (f32[1,256]{1,0:T(1,128)S(1)}, f32[1,256]{1,0:T(1,128)S(1)}, u32[]{:S(2)}, u32[]{:S(2)}) collective-permute-start(f32[1,256]{1,0:T(1,128)S(1)} %shard_map.30), channel_id=1, source_target_pairs={{0,4},{4,0},{1,5},{5,1},{2,6},{6,2},{3,7},{7,3},{8,12},{12,8},{9,1... | collective-permute-start | bytes 3080 | tf_op jit(solution)/shard_map/ppermute | solution.py:161
  61.3 0.6 shard_map.29
  61.9 0.1 collective-permute-done.4
  62.1 0.1 reshape.27
  62.2 17.3 %all_to_all.11 = f32[128,1,2]{2,1,0:T(1,128)S(1)} all-to-all(f32[128,1,2]{2,1,0:T(1,128)S(1)} %bitcast.6), channel_id=1, replica_groups=mesh['chip'=64,'core'=2,'far'=2,'near'=2] {'chip','near'}, dimensions={0} | all-to-all | bytes 2048 | tf_op jit(solution)/shard_map/all_to_all | solution.py:181
  79.5 0.6 shard_map.31
  (5 shorter events, 0.0 us)
Async XLA Ops:
  0.0 0.7 copy-start.1
  0.7 0.9 %copy-start = (bf16[128,1024]{1,0:T(8,128)(2,1)S(1)}, bf16[128,1024]{1,0:T(8,128)(2,1)}, u32[]{:S(2)}) copy-start(bf16[128,1024]{1,0:T(8,128)(2,1)} %emb_ref.1) | copy-start | bytes 786436
  39.3 18.0 %collective-permute-start.1 = (bf16[256,1024]{1,0:T(8,128)(2,1)S(1)}, bf16[256,1024]{1,0:T(8,128)(2,1)S(1)}, u32[]{:S(2)}, u32[]{:S(2)}) collective-permute-start(bf16[256,1024]{1,0:T(8,128)(2,1)S(1)} %slice.12), channel_id=1, source_target_pairs={{0,3},{1,2},{2,1},{3,0},{4,7},{5,6},{6,5},{7,4},{8,11},{9,10},{10,... | collective-permute-start | bytes 1572872 | tf_op jit(solution)/shard_map/ppermute | solution.py:165
  44.6 12.7 %collective-permute-start = (bf16[256,1024]{1,0:T(8,128)(2,1)S(1)}, bf16[256,1024]{1,0:T(8,128)(2,1)S(1)}, u32[]{:S(2)}, u32[]{:S(2)}) collective-permute-start(bf16[256,1024]{1,0:T(8,128)(2,1)S(1)} %slice.12), channel_id=1, source_target_pairs={{0,4},{4,0},{1,5},{5,1},{2,6},{6,2},{3,7},{7,3},{8,12},{12,8},{9,1... | collective-permute-start | bytes 1572872 | tf_op jit(solution)/shard_map/ppermute | solution.py:161
  49.9 4.1 %collective-permute-start.2 = (bf16[256]{0:T(256)(128)(2,1)S(1)}, bf16[256]{0:T(256)(128)(2,1)S(1)}, u32[]{:S(2)}, u32[]{:S(2)}) collective-permute-start(bf16[256]{0:T(256)(128)(2,1)S(1)} %slice_reduce_fusion), channel_id=1, source_target_pairs={{0,4},{4,0},{1,5},{5,1},{2,6},{6,2},{3,7},{7,3},{8,12},{12,8},{9,1... | collective-permute-start | bytes 1544 | tf_op jit(solution)/shard_map/ppermute | solution.py:161
  51.8 5.5 %collective-permute-start.3 = (bf16[256]{0:T(256)(128)(2,1)S(1)}, bf16[256]{0:T(256)(128)(2,1)S(1)}, u32[]{:S(2)}, u32[]{:S(2)}) collective-permute-start(bf16[256]{0:T(256)(128)(2,1)S(1)} %slice_reduce_fusion), channel_id=1, source_target_pairs={{0,3},{1,2},{2,1},{3,0},{4,7},{5,6},{6,5},{7,4},{8,11},{9,10},{10,... | collective-permute-start | bytes 1544 | tf_op jit(solution)/shard_map/ppermute | solution.py:165
  57.7 4.4 %collective-permute-start.4 = (f32[1,256]{1,0:T(1,128)S(1)}, f32[1,256]{1,0:T(1,128)S(1)}, u32[]{:S(2)}, u32[]{:S(2)}) collective-permute-start(f32[1,256]{1,0:T(1,128)S(1)} %shard_map.30), channel_id=1, source_target_pairs={{0,4},{4,0},{1,5},{5,1},{2,6},{6,2},{3,7},{7,3},{8,12},{12,8},{9,1... | collective-permute-start | bytes 3080 | tf_op jit(solution)/shard_map/ppermute | solution.py:161

commit v8 on v7

--- a/solution.py
+++ b/solution.py
@@ -10,6 +10,7 @@
 META = 128
 AXES = ("chip", "core", "far", "near")
 PEERS = ("chip", "near")
+BOTH = ("core",) + PEERS
 VMEM = pl.BlockSpec(memory_space=pltpu.VMEM)
 ROOM = pltpu.CompilerParams(vmem_limit_bytes=16 * 1024 * 1024)
 
@@ -59,8 +60,8 @@
 
 def take_kernel(slot_ref, answer_ref, out_ref):
     slot = slot_ref[...]
-    answer = answer_ref[...]
-    owners = answer.shape[0]
+    owners = answer_ref.shape[0] // 2
+    answer = jnp.maximum(answer_ref[:owners, :], answer_ref[owners:, :])
     chosen = jnp.where((slot & 1) == 0, answer[:, 0:1], answer[:, 1:2])
     here = (slot >> 1) == lax.broadcasted_iota(jnp.int32, (owners, slot.shape[1]), 0)
     out_ref[...] = jnp.sum(jnp.where(here, chosen, 0.0), axis=0, keepdims=True)
@@ -101,60 +102,65 @@
     return jnp.transpose(row)[:, 0:1]
 
 
-def lent_kernel(head_ref, beyond_ref, beyond_mark_ref, twin_ref, twin_mark_ref, out_ref):
-    core, far = lax.axis_index("core"), lax.axis_index("far")
-    key = jnp.concatenate([head_ref[...], beyond_ref[HEAD:, :]], axis=0)
-    out_ref[...] = found(
-        key,
-        row_column(beyond_mark_ref),
-        (core, 1 - far),
-        twin_ref[...],
-        twin_mark_ref[...].astype(jnp.float32),
-        (1 - core, far),
-    )
-
-
-def lend(beyond, beyond_mark, twin, twin_mark):
-    slots, width = beyond.shape
-    return pl.pallas_call(
-        lent_kernel,
+def own_kernel(recv_ref, mark_ref, out_ref):
+    at = (lax.axis_index("core"), lax.axis_index("far"))
+    rows = recv_ref[:, :-META]
+    out_ref[...] = found(rows, column(recv_ref), at, rows, mark_ref[...].astype(jnp.float32), at)
+
+
+def best_own(recv, mark):
+    slots = recv.shape[0]
+    return pl.pallas_call(
+        own_kernel,
         out_shape=jax.ShapeDtypeStruct((1, slots), jnp.float32),
-        in_specs=[VMEM] * 5,
+        in_specs=[VMEM] * 2,
         out_specs=VMEM,
         compiler_params=ROOM,
         cost_estimate=pl.CostEstimate(
-            flops=2 * slots * slots * width, bytes_accessed=4 * slots * width, transcendentals=0
+            flops=2 * slots * slots * 1024, bytes_accessed=4 * slots * 1024, transcendentals=0
         ),
-    )(beyond[:HEAD], beyond, beyond_mark.reshape(1, slots), twin, twin_mark.reshape(1, slots))
-
-
-def mine_kernel(
-    recv_ref, twin_ref, beyond_ref, mark_ref, twin_mark_ref, beyond_mark_ref, out_ref
+    )(recv, mark.reshape(1, slots))
+
+
+def score_kernel(
+    recv_ref,
+    own_ref,
+    twin_ref,
+    head_ref,
+    beyond_ref,
+    mark_ref,
+    twin_mark_ref,
+    beyond_mark_ref,
+    out_ref,
 ):
     core, far = lax.axis_index("core"), lax.axis_index("far")
-    query = recv_ref[:, :-META]
+    slots = recv_ref.shape[0]
+    at, twin_at, beyond_at = (core, far), (1 - core, far), (core, 1 - far)
+    query, twin = recv_ref[:, :-META], twin_ref[...]
     mark = mark_ref[...].astype(jnp.float32)
-    at = (core, far)
-    best = found(query, column(recv_ref), at, query, mark, at)
-    twin = found(twin_ref[...], row_column(twin_mark_ref), (1 - core, far), query, mark, at)
-    beyond = found(
-        beyond_ref[...], row_column(beyond_mark_ref), (core, 1 - far), query, mark, at
-    )
-    out_ref[...] = jnp.maximum(best, jnp.maximum(twin, beyond))
-
-
-def best_of_mine(recv, twin, beyond, *marks):
+    twin_mark = twin_mark_ref[...].astype(jnp.float32)
+    beyond = jnp.concatenate([head_ref[...], beyond_ref[HEAD:, :]], axis=0)
+    beyond_mark = row_column(beyond_mark_ref)
+    mine = own_ref[...]
+    mine = jnp.maximum(mine, found(twin, row_column(twin_mark_ref), twin_at, query, mark, at))
+    mine = jnp.maximum(mine, found(beyond, beyond_mark, beyond_at, query, mark, at))
+    lent = found(beyond, beyond_mark, beyond_at, twin, twin_mark, twin_at)
+    row = lax.broadcasted_iota(jnp.int32, (2, slots), 0)
+    out_ref[...] = jnp.where(row == core, mine, lent)
+
+
+def best_scores(recv, own, twin, beyond, *marks):
     slots, width = beyond.shape
     return pl.pallas_call(
-        mine_kernel,
-        out_shape=jax.ShapeDtypeStruct((1, slots), jnp.float32),
-        in_specs=[VMEM] * 6,
+        score_kernel,
+        out_shape=jax.ShapeDtypeStruct((2, slots), jnp.float32),
+        in_specs=[VMEM] * 8,
         out_specs=VMEM,
         compiler_params=ROOM,
         cost_estimate=pl.CostEstimate(
             flops=6 * slots * slots * width, bytes_accessed=6 * slots * width, transcendentals=0
         ),
-    )(recv, twin, beyond, *(m.reshape(1, slots) for m in marks))
+    )(recv, own, twin, beyond[:HEAD], beyond, *(m.reshape(1, slots) for m in marks))
 
 
 def swap(value, axis):
@@ -176,12 +182,13 @@
     rows, mark = recv[:, :width], recv[:, width]
     far_rows, far_mark = cross(rows), cross(mark)
     twin, twin_mark = swap(rows, "core"), swap(mark, "core")
-    lent = swap(lend(far_rows, far_mark, twin, twin_mark), "core")
-    nearest = jnp.maximum(best_of_mine(recv, twin, far_rows, mark, twin_mark, far_mark), lent)
+    best = best_scores(
+        recv, best_own(recv, mark), twin, far_rows, mark, twin_mark, far_mark
+    )
     answer = lax.all_to_all(
-        nearest.reshape(peers, 1, 2), PEERS, split_axis=0, concat_axis=0, tiled=True
-    )
-    return take(slot, answer.reshape(peers, 2))
+        best.reshape(2 * peers, 1, 2), BOTH, split_axis=0, concat_axis=0, tiled=True
+    )
+    return take(slot, answer.reshape(2 * peers, 2))
 
 
 def solution(mesh):

time: 81.2 us -> 81.6 us (level)
  blocking collectives: 54.3 us -> 59.5 us
  starting transfers between devices: 18 us -> 14.5 us
    all_to_all x1, blocking collectives: 17.3 us -> 22.5 us  [per_device(): lax.all_to_all(best.reshape(2 * peers, 1, 2), BOTH, split_axis=0, concat_...]
    ppermute x3 -> x2, starting transfers between devices: 10.7 us -> 7.11 us  [swap(): return lax.ppermute(value, axis, [(0, 1), (1, 0)])]
  transfers between devices with their start and end apart: 5 -> 4, of which waited for: 2 -> 1; matrix products, arithmetic and copies ran while one was open for 0% -> 0% of each run, Pallas kernels for 1% -> 0%
where the time goes in v8:
time: 81.6 us; the launch traced here: 81.3 us
  blocking collectives  59.5 us (73%)
  starting transfers between devices  14.5 us (18%)
  waiting for transfers between devices  3.02 us (4%)
  local copies, waits for them, and re-layouts  2.15 us (3%)
  Pallas kernels  2.06 us (3%)
    all_to_all x1, blocking collectives, per_device(): lax.all_to_all(send, PEERS, split_axis=0, concat_axis=0, tiled=True)  37 us
    all_to_all x1, blocking collectives, per_device(): lax.all_to_all(best.reshape(2 * peers, 1, 2), BOTH, split_axis=0, concat_...  22.5 us
    ppermute x2, starting transfers between devices, cross(): return lax.ppermute(value, ('far', 'near'), [(x, 3 - x) for x in range(4)])  7.35 us
    ppermute x2, starting transfers between devices, swap(): return lax.ppermute(value, axis, [(0, 1), (1, 0)])  7.11 us
    ppermute x2, waiting for transfers between devices, cross(): return lax.ppermute(value, ('far', 'near'), [(x, 3 - x) for x in range(4)])  3.02 us
  transfers between devices with their start and end apart: 4, of which 1 were waited for; matrix products, arithmetic and copies ran while one was open for 0% of the time, Pallas kernels for 0%

profile of v8, /device:TPU:1, one launch (start us, length us, event | category | flops | bytes accessed | tf_op | source)
XLA Modules:
  0.0 81.3 jit_solution(843930212058738798)
XLA Ops:
  0.0 0.0 copy-start.1
  0.0 0.7 copy-done.1
  0.7 0.0 copy-start
  0.7 0.9 %copy-done = bf16[128,1024]{1,0:T(8,128)(2,1)S(1)} copy-done((bf16[128,1024]{1,0:T(8,128)(2,1)S(1)}, bf16[128,1024]{1,0:T(8,128)(2,1)}, u32[]{:S(2)}) %copy-start) | copy-done | bytes 262168
  1.6 0.4 shard_map.28
  2.1 37.0 %all_to_all.10 = bf16[128,2,1152]{2,1,0:T(2,128)(2,1)S(1)} all-to-all(bf16[128,2,1152]{2,1,0:T(2,128)(2,1)S(1)} %get-tuple-element.8), channel_id=1, replica_groups=mesh['chip'=64,'core'=2,'far'=2,'near'=2] {'chip','near'}, dimensions={0} | all-to-all | bytes 1179648 | tf_op jit(solution)/shard_map/all_to_all | solution.py:179
  39.0 0.2 reshape.22.recv_ref
  39.3 0.1 slice.13
  39.3 5.2 %collective-permute-start.1 = (bf16[256,1024]{1,0:T(8,128)(2,1)S(1)}, bf16[256,1024]{1,0:T(8,128)(2,1)S(1)}, u32[]{:S(2)}, u32[]{:S(2)}) collective-permute-start(bf16[256,1024]{1,0:T(8,128)(2,1)S(1)} %slice.13), channel_id=1, source_target_pairs={{0,3},{1,2},{2,1},{3,0},{4,7},{5,6},{6,5},{7,4},{8,11},{9,10},{10,... | collective-permute-start | bytes 1572872 | tf_op jit(solution)/shard_map/ppermute | solution.py:171
  44.6 5.2 %collective-permute-start = (bf16[256,1024]{1,0:T(8,128)(2,1)S(1)}, bf16[256,1024]{1,0:T(8,128)(2,1)S(1)}, u32[]{:S(2)}, u32[]{:S(2)}) collective-permute-start(bf16[256,1024]{1,0:T(8,128)(2,1)S(1)} %slice.13), channel_id=1, source_target_pairs={{0,4},{4,0},{1,5},{5,1},{2,6},{6,2},{3,7},{7,3},{8,12},{12,8},{9,1... | collective-permute-start | bytes 1572872 | tf_op jit(solution)/shard_map/ppermute | solution.py:167
  49.8 0.1 slice_reduce_fusion
  49.9 1.9 %collective-permute-start.2 = (bf16[256]{0:T(256)(128)(2,1)S(1)}, bf16[256]{0:T(256)(128)(2,1)S(1)}, u32[]{:S(2)}, u32[]{:S(2)}) collective-permute-start(bf16[256]{0:T(256)(128)(2,1)S(1)} %slice_reduce_fusion), channel_id=1, source_target_pairs={{0,4},{4,0},{1,5},{5,1},{2,6},{6,2},{3,7},{7,3},{8,12},{12,8},{9,1... | collective-permute-start | bytes 1544 | tf_op jit(solution)/shard_map/ppermute | solution.py:167
  51.8 2.1 %collective-permute-start.3 = (bf16[256]{0:T(256)(128)(2,1)S(1)}, bf16[256]{0:T(256)(128)(2,1)S(1)}, u32[]{:S(2)}, u32[]{:S(2)}) collective-permute-start(bf16[256]{0:T(256)(128)(2,1)S(1)} %slice_reduce_fusion), channel_id=1, source_target_pairs={{0,3},{1,2},{2,1},{3,0},{4,7},{5,6},{6,5},{7,4},{8,11},{9,10},{10,... | collective-permute-start | bytes 1544 | tf_op jit(solution)/shard_map/ppermute | solution.py:171
  53.9 0.3 shard_map.29.own_ref
  54.3 0.0 collective-permute-done.2
  54.3 3.0 %collective-permute-done.3 = bf16[256]{0:T(256)(128)(2,1)S(1)} collective-permute-done((bf16[256]{0:T(256)(128)(2,1)S(1)}, bf16[256]{0:T(256)(128)(2,1)S(1)}, u32[]{:S(2)}, u32[]{:S(2)}) %collective-permute-start.3) | collective-permute-done | bytes 544 | tf_op jit(solution)/shard_map/ppermute | solution.py:171
  57.3 0.0 collective-permute-done.1.beyond_ref
  57.3 0.0 collective-permute-done.twin_ref
  57.4 0.7 shard_map.30
  58.0 0.1 reshape.25
  58.2 22.5 %all_to_all.11 = f32[256,1,2]{2,1,0:T(1,128)S(1)} all-to-all(f32[256,1,2]{2,1,0:T(1,128)S(1)} %bitcast.6), channel_id=1, replica_groups=mesh['chip'=64,'core'=2,'far'=2,'near'=2] {'core','chip','near'}, dimensions={0} | all-to-all | bytes 4096 | tf_op jit(solution)/shard_map/all_to_all | solution.py:188
  80.7 0.6 shard_map.31
  (4 shorter events, 0.0 us)
Async XLA Ops:
  0.0 0.7 copy-start.1
  0.7 0.9 %copy-start = (bf16[128,1024]{1,0:T(8,128)(2,1)S(1)}, bf16[128,1024]{1,0:T(8,128)(2,1)}, u32[]{:S(2)}) copy-start(bf16[128,1024]{1,0:T(8,128)(2,1)} %emb_ref.1) | copy-start | bytes 786436
  39.3 18.0 %collective-permute-start.1 = (bf16[256,1024]{1,0:T(8,128)(2,1)S(1)}, bf16[256,1024]{1,0:T(8,128)(2,1)S(1)}, u32[]{:S(2)}, u32[]{:S(2)}) collective-permute-start(bf16[256,1024]{1,0:T(8,128)(2,1)S(1)} %slice.13), channel_id=1, source_target_pairs={{0,3},{1,2},{2,1},{3,0},{4,7},{5,6},{6,5},{7,4},{8,11},{9,10},{10,... | collective-permute-start | bytes 1572872 | tf_op jit(solution)/shard_map/ppermute | solution.py:171
  44.6 12.8 %collective-permute-start = (bf16[256,1024]{1,0:T(8,128)(2,1)S(1)}, bf16[256,1024]{1,0:T(8,128)(2,1)S(1)}, u32[]{:S(2)}, u32[]{:S(2)}) collective-permute-start(bf16[256,1024]{1,0:T(8,128)(2,1)S(1)} %slice.13), channel_id=1, source_target_pairs={{0,4},{4,0},{1,5},{5,1},{2,6},{6,2},{3,7},{7,3},{8,12},{12,8},{9,1... | collective-permute-start | bytes 1572872 | tf_op jit(solution)/shard_map/ppermute | solution.py:167
  49.9 4.4 %collective-permute-start.2 = (bf16[256]{0:T(256)(128)(2,1)S(1)}, bf16[256]{0:T(256)(128)(2,1)S(1)}, u32[]{:S(2)}, u32[]{:S(2)}) collective-permute-start(bf16[256]{0:T(256)(128)(2,1)S(1)} %slice_reduce_fusion), channel_id=1, source_target_pairs={{0,4},{4,0},{1,5},{5,1},{2,6},{6,2},{3,7},{7,3},{8,12},{12,8},{9,1... | collective-permute-start | bytes 1544 | tf_op jit(solution)/shard_map/ppermute | solution.py:167
  51.8 5.5 %collective-permute-start.3 = (bf16[256]{0:T(256)(128)(2,1)S(1)}, bf16[256]{0:T(256)(128)(2,1)S(1)}, u32[]{:S(2)}, u32[]{:S(2)}) collective-permute-start(bf16[256]{0:T(256)(128)(2,1)S(1)} %slice_reduce_fusion), channel_id=1, source_target_pairs={{0,3},{1,2},{2,1},{3,0},{4,7},{5,6},{6,5},{7,4},{8,11},{9,10},{10,... | collective-permute-start | bytes 1544 | tf_op jit(solution)/shard_map/ppermute | solution.py:171

commit v9 on v7

--- a/solution.py
+++ b/solution.py
@@ -8,8 +8,8 @@
 CL_DEV = 48
 EPSILON = 1e-06
 META = 128
-AXES = ("chip", "core", "far", "near")
-PEERS = ("chip", "near")
+AXES = ("z2", "z1", "z0", "y2", "y1", "y0", "core", "far", "near")
+PEERS = ("z0", "y0", "z1", "y1", "z2", "y2", "near")
 VMEM = pl.BlockSpec(memory_space=pltpu.VMEM)
 ROOM = pltpu.CompilerParams(vmem_limit_bytes=16 * 1024 * 1024)
 
@@ -82,8 +82,12 @@
     )
 
     def order(axis, at):
-        slot = lax.broadcasted_iota(jnp.int32, scores.shape, axis)
-        return (slot >> 2) * 16 + (slot & 3) + (at[0] * 8 + at[1] * 4)
+        shape = tuple(n if d == axis else 1 for d, n in enumerate(scores.shape))
+        slot = lax.broadcasted_iota(jnp.int32, shape, axis)
+        place = (slot & 1) + (at[0] * 8 + at[1] * 4)
+        for bit, name in enumerate(reversed(PEERS)):
+            place += ((slot >> (bit + 1)) & 1) << (len(AXES) - AXES.index(name))
+        return place
 
     allowed = (key_mark == query_mark) & (order(0, key_at) < order(1, query_at))
     return jnp.max(jnp.where(allowed, scores, -1.0), axis=0, keepdims=True)
@@ -167,7 +171,7 @@
 
 def per_device(embeddings, cluster_ids):
     docs, width = embeddings.shape
-    peers = lax.axis_size("chip") * lax.axis_size("near")
+    peers = lax.axis_size(PEERS)
     slots = 2 * peers
     send, slot = place(embeddings, cluster_ids, slots)
     recv = lax.all_to_all(
@@ -185,7 +189,7 @@
 
 
 def solution(mesh):
-    fine = Mesh(mesh.devices.reshape(mesh.shape["wide"] // 2, 2, 2, 2), AXES)
+    fine = Mesh(mesh.devices.reshape((2,) * len(AXES)), AXES)
     return jax.shard_map(
         per_device,
         mesh=fine,

time: 81.2 us -> 81 us (level)
  blocking collectives: 54.3 us -> 56.2 us
  starting transfers between devices: 18 us -> 16.6 us
  waiting for transfers between devices: 3.5 us -> 2.67 us
    all_to_all x1, blocking collectives: 37 us -> 38.1 us  [per_device(): lax.all_to_all(send, PEERS, split_axis=0, concat_axis=0, tiled=True)]
    ppermute x3, starting transfers between devices: 10.7 us -> 9.69 us  [swap(): return lax.ppermute(value, axis, [(0, 1), (1, 0)])]
    all_to_all x1, blocking collectives: 17.3 us -> 18.1 us  [per_device(): lax.all_to_all(nearest.reshape(peers, 1, 2), PEERS, split_axis=0, concat_...]
where the time goes in v9:
time: 81 us; the launch traced here: 80 us
  blocking collectives  56.2 us (69%)
  starting transfers between devices  16.6 us (20%)
  waiting for transfers between devices  2.67 us (3%)
  Pallas kernels  2.22 us (3%)
  local copies, waits for them, and re-layouts  2.14 us (3%)
    all_to_all x1, blocking collectives, per_device(): lax.all_to_all(send, PEERS, split_axis=0, concat_axis=0, tiled=True)  38.1 us
    all_to_all x1, blocking collectives, per_device(): lax.all_to_all(nearest.reshape(peers, 1, 2), PEERS, split_axis=0, concat_...  18.1 us
    ppermute x3, starting transfers between devices, swap(): return lax.ppermute(value, axis, [(0, 1), (1, 0)])  9.69 us
    ppermute x2, starting transfers between devices, cross(): return lax.ppermute(value, ('far', 'near'), [(x, 3 - x) for x in range(4)])  6.94 us
    ppermute x2, waiting for transfers between devices, cross(): return lax.ppermute(value, ('far', 'near'), [(x, 3 - x) for x in range(4)])  2.61 us
  transfers between devices with their start and end apart: 5, of which 2 were waited for; matrix products, arithmetic and copies ran while one was open for 0% of the time, Pallas kernels for 1%

profile of v9, /device:TPU:1, one launch (start us, length us, event | category | flops | bytes accessed | tf_op | source)
XLA Modules:
  0.0 80.0 jit_solution(822677390676979462)
XLA Ops:
  0.0 0.0 copy-start.1
  0.0 0.7 copy-done.1
  0.7 0.0 copy-start
  0.7 0.9 %copy-done = bf16[128,1024]{1,0:T(8,128)(2,1)S(1)} copy-done((bf16[128,1024]{1,0:T(8,128)(2,1)S(1)}, bf16[128,1024]{1,0:T(8,128)(2,1)}, u32[]{:S(2)}) %copy-start) | copy-done | bytes 262168
  1.6 0.4 shard_map.28
  2.1 38.1 %all_to_all.10 = bf16[128,2,1152]{2,1,0:T(2,128)(2,1)S(1)} all-to-all(bf16[128,2,1152]{2,1,0:T(2,128)(2,1)S(1)} %get-tuple-element.8), channel_id=1, replica_groups=mesh['z2'=2,'z1'=2,'z0'=2,'y2'=2,'y1'=2,'y0'=2,'core'=2,'far'=2,'near'=2..., dimensions={0} | all-to-all | bytes 1179648 | tf_op jit(solution)/shard_map/all_to_all | solution.py:177
  40.1 0.2 reshape.24.recv_ref
  40.4 0.1 slice.12
  40.4 3.7 %collective-permute-start.1 = (bf16[256,1024]{1,0:T(8,128)(2,1)S(1)}, bf16[256,1024]{1,0:T(8,128)(2,1)S(1)}, u32[]{:S(2)}, u32[]{:S(2)}) collective-permute-start(bf16[256,1024]{1,0:T(8,128)(2,1)S(1)} %slice.12), channel_id=1, source_target_pairs={{0,3},{1,2},{2,1},{3,0},{4,7},{5,6},{6,5},{7,4},{8,11},{9,10},{10,... | collective-permute-start | bytes 1572872 | tf_op jit(solution)/shard_map/ppermute | solution.py:169
  44.2 4.3 %collective-permute-start = (bf16[256,1024]{1,0:T(8,128)(2,1)S(1)}, bf16[256,1024]{1,0:T(8,128)(2,1)S(1)}, u32[]{:S(2)}, u32[]{:S(2)}) collective-permute-start(bf16[256,1024]{1,0:T(8,128)(2,1)S(1)} %slice.12), channel_id=1, source_target_pairs={{0,4},{4,0},{1,5},{5,1},{2,6},{6,2},{3,7},{7,3},{8,12},{12,8},{9,1... | collective-permute-start | bytes 1572872 | tf_op jit(solution)/shard_map/ppermute | solution.py:165
  48.5 0.1 slice_reduce_fusion
  48.6 1.9 %collective-permute-start.2 = (bf16[256]{0:T(256)(128)(2,1)S(1)}, bf16[256]{0:T(256)(128)(2,1)S(1)}, u32[]{:S(2)}, u32[]{:S(2)}) collective-permute-start(bf16[256]{0:T(256)(128)(2,1)S(1)} %slice_reduce_fusion), channel_id=1, source_target_pairs={{0,4},{4,0},{1,5},{5,1},{2,6},{6,2},{3,7},{7,3},{8,12},{12,8},{9,1... | collective-permute-start | bytes 1544 | tf_op jit(solution)/shard_map/ppermute | solution.py:165
  50.6 3.2 %collective-permute-start.3 = (bf16[256]{0:T(256)(128)(2,1)S(1)}, bf16[256]{0:T(256)(128)(2,1)S(1)}, u32[]{:S(2)}, u32[]{:S(2)}) collective-permute-start(bf16[256]{0:T(256)(128)(2,1)S(1)} %slice_reduce_fusion), channel_id=1, source_target_pairs={{0,3},{1,2},{2,1},{3,0},{4,7},{5,6},{6,5},{7,4},{8,11},{9,10},{10,... | collective-permute-start | bytes 1544 | tf_op jit(solution)/shard_map/ppermute | solution.py:169
  53.8 0.0 collective-permute-done.2
  53.8 2.6 %collective-permute-done.3 = bf16[256]{0:T(256)(128)(2,1)S(1)} collective-permute-done((bf16[256]{0:T(256)(128)(2,1)S(1)}, bf16[256]{0:T(256)(128)(2,1)S(1)}, u32[]{:S(2)}, u32[]{:S(2)}) %collective-permute-start.3) | collective-permute-done | bytes 544 | tf_op jit(solution)/shard_map/ppermute | solution.py:169
  56.4 0.0 collective-permute-done.1.beyond_ref
  56.4 0.0 collective-permute-done.twin_ref
  56.4 0.4 shard_map.30
  56.9 3.4 %collective-permute-start.4 = (f32[1,256]{1,0:T(1,128)S(1)}, f32[1,256]{1,0:T(1,128)S(1)}, u32[]{:S(2)}, u32[]{:S(2)}) collective-permute-start(f32[1,256]{1,0:T(1,128)S(1)} %shard_map.30), channel_id=1, source_target_pairs={{0,4},{4,0},{1,5},{5,1},{2,6},{6,2},{3,7},{7,3},{8,12},{12,8},{9,1... | collective-permute-start | bytes 3080 | tf_op jit(solution)/shard_map/ppermute | solution.py:165
  60.3 0.7 shard_map.29
  61.0 0.1 collective-permute-done.4
  61.1 0.1 reshape.27
  61.2 18.1 %all_to_all.11 = f32[128,1,2]{2,1,0:T(1,128)S(1)} all-to-all(f32[128,1,2]{2,1,0:T(1,128)S(1)} %bitcast.6), channel_id=1, replica_groups=mesh['z2'=2,'z1'=2,'z0'=2,'y2'=2,'y1'=2,'y0'=2,'core'=2,'far'=2,'near'=2..., dimensions={0} | all-to-all | bytes 2048 | tf_op jit(solution)/shard_map/all_to_all | solution.py:185
  79.4 0.6 shard_map.31
  (5 shorter events, 0.0 us)
Async XLA Ops:
  0.0 0.7 copy-start.1
  0.7 0.9 %copy-start = (bf16[128,1024]{1,0:T(8,128)(2,1)S(1)}, bf16[128,1024]{1,0:T(8,128)(2,1)}, u32[]{:S(2)}) copy-start(bf16[128,1024]{1,0:T(8,128)(2,1)} %emb_ref.1) | copy-start | bytes 786436
  40.4 16.0 %collective-permute-start.1 = (bf16[256,1024]{1,0:T(8,128)(2,1)S(1)}, bf16[256,1024]{1,0:T(8,128)(2,1)S(1)}, u32[]{:S(2)}, u32[]{:S(2)}) collective-permute-start(bf16[256,1024]{1,0:T(8,128)(2,1)S(1)} %slice.12), channel_id=1, source_target_pairs={{0,3},{1,2},{2,1},{3,0},{4,7},{5,6},{6,5},{7,4},{8,11},{9,10},{10,... | collective-permute-start | bytes 1572872 | tf_op jit(solution)/shard_map/ppermute | solution.py:169
  44.2 12.3 %collective-permute-start = (bf16[256,1024]{1,0:T(8,128)(2,1)S(1)}, bf16[256,1024]{1,0:T(8,128)(2,1)S(1)}, u32[]{:S(2)}, u32[]{:S(2)}) collective-permute-start(bf16[256,1024]{1,0:T(8,128)(2,1)S(1)} %slice.12), channel_id=1, source_target_pairs={{0,4},{4,0},{1,5},{5,1},{2,6},{6,2},{3,7},{7,3},{8,12},{12,8},{9,1... | collective-permute-start | bytes 1572872 | tf_op jit(solution)/shard_map/ppermute | solution.py:165
  48.6 5.2 %collective-permute-start.2 = (bf16[256]{0:T(256)(128)(2,1)S(1)}, bf16[256]{0:T(256)(128)(2,1)S(1)}, u32[]{:S(2)}, u32[]{:S(2)}) collective-permute-start(bf16[256]{0:T(256)(128)(2,1)S(1)} %slice_reduce_fusion), channel_id=1, source_target_pairs={{0,4},{4,0},{1,5},{5,1},{2,6},{6,2},{3,7},{7,3},{8,12},{12,8},{9,1... | collective-permute-start | bytes 1544 | tf_op jit(solution)/shard_map/ppermute | solution.py:165
  50.6 5.9 %collective-permute-start.3 = (bf16[256]{0:T(256)(128)(2,1)S(1)}, bf16[256]{0:T(256)(128)(2,1)S(1)}, u32[]{:S(2)}, u32[]{:S(2)}) collective-permute-start(bf16[256]{0:T(256)(128)(2,1)S(1)} %slice_reduce_fusion), channel_id=1, source_target_pairs={{0,3},{1,2},{2,1},{3,0},{4,7},{5,6},{6,5},{7,4},{8,11},{9,10},{10,... | collective-permute-start | bytes 1544 | tf_op jit(solution)/shard_map/ppermute | solution.py:169
  56.9 4.2 %collective-permute-start.4 = (f32[1,256]{1,0:T(1,128)S(1)}, f32[1,256]{1,0:T(1,128)S(1)}, u32[]{:S(2)}, u32[]{:S(2)}) collective-permute-start(f32[1,256]{1,0:T(1,128)S(1)} %shard_map.30), channel_id=1, source_target_pairs={{0,4},{4,0},{1,5},{5,1},{2,6},{6,2},{3,7},{7,3},{8,12},{12,8},{9,1... | collective-permute-start | bytes 3080 | tf_op jit(solution)/shard_map/ppermute | solution.py:165

commit v10 on v9

--- a/solution.py
+++ b/solution.py
@@ -9,7 +9,7 @@
 EPSILON = 1e-06
 META = 128
 AXES = ("z2", "z1", "z0", "y2", "y1", "y0", "core", "far", "near")
-PEERS = ("z0", "y0", "z1", "y1", "z2", "y2", "near")
+PEERS = ("y0", "z0", "y1", "z1", "y2", "z2", "near")
 VMEM = pl.BlockSpec(memory_space=pltpu.VMEM)
 ROOM = pltpu.CompilerParams(vmem_limit_bytes=16 * 1024 * 1024)
 

time: 81 us -> 80.1 us (0.989)
  blocking collectives: 56.2 us -> 54.4 us
  starting transfers between devices: 16.6 us -> 17.6 us
    all_to_all x1, blocking collectives: 38.1 us -> 36.7 us  [per_device(): lax.all_to_all(send, PEERS, split_axis=0, concat_axis=0, tiled=True)]
    ppermute x3, starting transfers between devices: 9.69 us -> 11 us  [swap(): return lax.ppermute(value, axis, [(0, 1), (1, 0)])]
where the time goes in v10:
time: 80.1 us; the launch traced here: 79.5 us
  blocking collectives  54.4 us (68%)
  starting transfers between devices  17.6 us (22%)
  waiting for transfers between devices  3.02 us (4%)
  Pallas kernels  2.22 us (3%)
  local copies, waits for them, and re-layouts  2.14 us (3%)
    all_to_all x1, blocking collectives, per_device(): lax.all_to_all(send, PEERS, split_axis=0, concat_axis=0, tiled=True)  36.7 us
    all_to_all x1, blocking collectives, per_device(): lax.all_to_all(nearest.reshape(peers, 1, 2), PEERS, split_axis=0, concat_...  17.7 us
    ppermute x3, starting transfers between devices, swap(): return lax.ppermute(value, axis, [(0, 1), (1, 0)])  11 us
    ppermute x2, starting transfers between devices, cross(): return lax.ppermute(value, ('far', 'near'), [(x, 3 - x) for x in range(4)])  6.58 us
    ppermute x2, waiting for transfers between devices, cross(): return lax.ppermute(value, ('far', 'near'), [(x, 3 - x) for x in range(4)])  2.96 us
    unnamed x4, local copies, waits for them, and re-layouts  1.6 us
  transfers between devices with their start and end apart: 5, of which 2 were waited for; matrix products, arithmetic and copies ran while one was open for 0% of the time, Pallas kernels for 1%

profile of v10, /device:TPU:1, one launch (start us, length us, event | category | flops | bytes accessed | tf_op | source)
XLA Modules:
  0.0 79.5 jit_solution(5405965698745455756)
XLA Ops:
  0.0 0.0 copy-start.1
  0.0 0.7 copy-done.1
  0.7 0.0 copy-start
  0.7 0.9 %copy-done = bf16[128,1024]{1,0:T(8,128)(2,1)S(1)} copy-done((bf16[128,1024]{1,0:T(8,128)(2,1)S(1)}, bf16[128,1024]{1,0:T(8,128)(2,1)}, u32[]{:S(2)}) %copy-start) | copy-done | bytes 262168
  1.6 0.4 shard_map.28
  2.1 36.7 %all_to_all.10 = bf16[128,2,1152]{2,1,0:T(2,128)(2,1)S(1)} all-to-all(bf16[128,2,1152]{2,1,0:T(2,128)(2,1)S(1)} %get-tuple-element.8), channel_id=1, replica_groups=mesh['z2'=2,'z1'=2,'z0'=2,'y2'=2,'y1'=2,'y0'=2,'core'=2,'far'=2,'near'=2..., dimensions={0} | all-to-all | bytes 1179648 | tf_op jit(solution)/shard_map/all_to_all | solution.py:177
  38.8 0.2 reshape.24.recv_ref
  39.0 0.1 slice.12
  39.1 4.1 %collective-permute-start.1 = (bf16[256,1024]{1,0:T(8,128)(2,1)S(1)}, bf16[256,1024]{1,0:T(8,128)(2,1)S(1)}, u32[]{:S(2)}, u32[]{:S(2)}) collective-permute-start(bf16[256,1024]{1,0:T(8,128)(2,1)S(1)} %slice.12), channel_id=1, source_target_pairs={{0,3},{1,2},{2,1},{3,0},{4,7},{5,6},{6,5},{7,4},{8,11},{9,10},{10,... | collective-permute-start | bytes 1572872 | tf_op jit(solution)/shard_map/ppermute | solution.py:169
  43.1 5.5 %collective-permute-start = (bf16[256,1024]{1,0:T(8,128)(2,1)S(1)}, bf16[256,1024]{1,0:T(8,128)(2,1)S(1)}, u32[]{:S(2)}, u32[]{:S(2)}) collective-permute-start(bf16[256,1024]{1,0:T(8,128)(2,1)S(1)} %slice.12), channel_id=1, source_target_pairs={{0,4},{4,0},{1,5},{5,1},{2,6},{6,2},{3,7},{7,3},{8,12},{12,8},{9,1... | collective-permute-start | bytes 1572872 | tf_op jit(solution)/shard_map/ppermute | solution.py:165
  48.7 0.1 slice_reduce_fusion
  48.8 1.9 %collective-permute-start.2 = (bf16[256]{0:T(256)(128)(2,1)S(1)}, bf16[256]{0:T(256)(128)(2,1)S(1)}, u32[]{:S(2)}, u32[]{:S(2)}) collective-permute-start(bf16[256]{0:T(256)(128)(2,1)S(1)} %slice_reduce_fusion), channel_id=1, source_target_pairs={{0,4},{4,0},{1,5},{5,1},{2,6},{6,2},{3,7},{7,3},{8,12},{12,8},{9,1... | collective-permute-start | bytes 1544 | tf_op jit(solution)/shard_map/ppermute | solution.py:165
  50.7 2.5 %collective-permute-start.3 = (bf16[256]{0:T(256)(128)(2,1)S(1)}, bf16[256]{0:T(256)(128)(2,1)S(1)}, u32[]{:S(2)}, u32[]{:S(2)}) collective-permute-start(bf16[256]{0:T(256)(128)(2,1)S(1)} %slice_reduce_fusion), channel_id=1, source_target_pairs={{0,3},{1,2},{2,1},{3,0},{4,7},{5,6},{6,5},{7,4},{8,11},{9,10},{10,... | collective-permute-start | bytes 1544 | tf_op jit(solution)/shard_map/ppermute | solution.py:169
  53.3 0.0 collective-permute-done.2
  53.3 3.0 %collective-permute-done.3 = bf16[256]{0:T(256)(128)(2,1)S(1)} collective-permute-done((bf16[256]{0:T(256)(128)(2,1)S(1)}, bf16[256]{0:T(256)(128)(2,1)S(1)}, u32[]{:S(2)}, u32[]{:S(2)}) %collective-permute-start.3) | collective-permute-done | bytes 544 | tf_op jit(solution)/shard_map/ppermute | solution.py:169
  56.2 0.0 collective-permute-done.1.beyond_ref
  56.2 0.0 collective-permute-done.twin_ref
  56.3 0.4 shard_map.30
  56.7 3.6 %collective-permute-start.4 = (f32[1,256]{1,0:T(1,128)S(1)}, f32[1,256]{1,0:T(1,128)S(1)}, u32[]{:S(2)}, u32[]{:S(2)}) collective-permute-start(f32[1,256]{1,0:T(1,128)S(1)} %shard_map.30), channel_id=1, source_target_pairs={{0,4},{4,0},{1,5},{5,1},{2,6},{6,2},{3,7},{7,3},{8,12},{12,8},{9,1... | collective-permute-start | bytes 3080 | tf_op jit(solution)/shard_map/ppermute | solution.py:165
  60.2 0.7 shard_map.29
  61.0 0.1 collective-permute-done.4
  61.1 0.1 reshape.27
  61.2 17.7 %all_to_all.11 = f32[128,1,2]{2,1,0:T(1,128)S(1)} all-to-all(f32[128,1,2]{2,1,0:T(1,128)S(1)} %bitcast.6), channel_id=1, replica_groups=mesh['z2'=2,'z1'=2,'z0'=2,'y2'=2,'y1'=2,'y0'=2,'core'=2,'far'=2,'near'=2..., dimensions={0} | all-to-all | bytes 2048 | tf_op jit(solution)/shard_map/all_to_all | solution.py:185
  78.9 0.6 shard_map.31
  (5 shorter events, 0.0 us)
Async XLA Ops:
  0.0 0.7 copy-start.1
  0.7 0.9 %copy-start = (bf16[128,1024]{1,0:T(8,128)(2,1)S(1)}, bf16[128,1024]{1,0:T(8,128)(2,1)}, u32[]{:S(2)}) copy-start(bf16[128,1024]{1,0:T(8,128)(2,1)} %emb_ref.1) | copy-start | bytes 786436
  39.1 17.2 %collective-permute-start.1 = (bf16[256,1024]{1,0:T(8,128)(2,1)S(1)}, bf16[256,1024]{1,0:T(8,128)(2,1)S(1)}, u32[]{:S(2)}, u32[]{:S(2)}) collective-permute-start(bf16[256,1024]{1,0:T(8,128)(2,1)S(1)} %slice.12), channel_id=1, source_target_pairs={{0,3},{1,2},{2,1},{3,0},{4,7},{5,6},{6,5},{7,4},{8,11},{9,10},{10,... | collective-permute-start | bytes 1572872 | tf_op jit(solution)/shard_map/ppermute | solution.py:169
  43.1 13.1 %collective-permute-start = (bf16[256,1024]{1,0:T(8,128)(2,1)S(1)}, bf16[256,1024]{1,0:T(8,128)(2,1)S(1)}, u32[]{:S(2)}, u32[]{:S(2)}) collective-permute-start(bf16[256,1024]{1,0:T(8,128)(2,1)S(1)} %slice.12), channel_id=1, source_target_pairs={{0,4},{4,0},{1,5},{5,1},{2,6},{6,2},{3,7},{7,3},{8,12},{12,8},{9,1... | collective-permute-start | bytes 1572872 | tf_op jit(solution)/shard_map/ppermute | solution.py:165
  48.8 4.4 %collective-permute-start.2 = (bf16[256]{0:T(256)(128)(2,1)S(1)}, bf16[256]{0:T(256)(128)(2,1)S(1)}, u32[]{:S(2)}, u32[]{:S(2)}) collective-permute-start(bf16[256]{0:T(256)(128)(2,1)S(1)} %slice_reduce_fusion), channel_id=1, source_target_pairs={{0,4},{4,0},{1,5},{5,1},{2,6},{6,2},{3,7},{7,3},{8,12},{12,8},{9,1... | collective-permute-start | bytes 1544 | tf_op jit(solution)/shard_map/ppermute | solution.py:165
  50.7 5.5 %collective-permute-start.3 = (bf16[256]{0:T(256)(128)(2,1)S(1)}, bf16[256]{0:T(256)(128)(2,1)S(1)}, u32[]{:S(2)}, u32[]{:S(2)}) collective-permute-start(bf16[256]{0:T(256)(128)(2,1)S(1)} %slice_reduce_fusion), channel_id=1, source_target_pairs={{0,3},{1,2},{2,1},{3,0},{4,7},{5,6},{6,5},{7,4},{8,11},{9,10},{10,... | collective-permute-start | bytes 1544 | tf_op jit(solution)/shard_map/ppermute | solution.py:169
  56.7 4.4 %collective-permute-start.4 = (f32[1,256]{1,0:T(1,128)S(1)}, f32[1,256]{1,0:T(1,128)S(1)}, u32[]{:S(2)}, u32[]{:S(2)}) collective-permute-start(f32[1,256]{1,0:T(1,128)S(1)} %shard_map.30), channel_id=1, source_target_pairs={{0,4},{4,0},{1,5},{5,1},{2,6},{6,2},{3,7},{7,3},{8,12},{12,8},{9,1... | collective-permute-start | bytes 3080 | tf_op jit(solution)/shard_map/ppermute | solution.py:165

commit v11 on v10

--- a/solution.py
+++ b/solution.py
@@ -9,7 +9,7 @@
 EPSILON = 1e-06
 META = 128
 AXES = ("z2", "z1", "z0", "y2", "y1", "y0", "core", "far", "near")
-PEERS = ("y0", "z0", "y1", "z1", "y2", "z2", "near")
+PEERS = ("y0", "y1", "y2", "z0", "z1", "z2", "near")
 VMEM = pl.BlockSpec(memory_space=pltpu.VMEM)
 ROOM = pltpu.CompilerParams(vmem_limit_bytes=16 * 1024 * 1024)
 

time: 80.1 us -> 80.3 us (level)
  blocking collectives: 54.4 us -> 55.3 us
where the time goes in v11:
time: 80.3 us; the launch traced here: 79.7 us
  blocking collectives  55.3 us (69%)
  starting transfers between devices  17.1 us (21%)
  waiting for transfers between devices  2.87 us (4%)
  Pallas kernels  2.22 us (3%)
  local copies, waits for them, and re-layouts  2.14 us (3%)
    all_to_all x1, blocking collectives, per_device(): lax.all_to_all(send, PEERS, split_axis=0, concat_axis=0, tiled=True)  37.1 us
    all_to_all x1, blocking collectives, per_device(): lax.all_to_all(nearest.reshape(peers, 1, 2), PEERS, split_axis=0, concat_...  18.2 us
    ppermute x3, starting transfers between devices, swap(): return lax.ppermute(value, axis, [(0, 1), (1, 0)])  10.5 us
    ppermute x2, starting transfers between devices, cross(): return lax.ppermute(value, ('far', 'near'), [(x, 3 - x) for x in range(4)])  6.59 us
    ppermute x2, waiting for transfers between devices, cross(): return lax.ppermute(value, ('far', 'near'), [(x, 3 - x) for x in range(4)])  2.81 us
  transfers between devices with their start and end apart: 5, of which 2 were waited for; matrix products, arithmetic and copies ran while one was open for 0% of the time, Pallas kernels for 1%

profile of v11, /device:TPU:1, one launch (start us, length us, event | category | flops | bytes accessed | tf_op | source)
XLA Modules:
  0.0 79.7 jit_solution(2740318526029510541)
XLA Ops:
  0.0 0.0 copy-start.1
  0.0 0.7 copy-done.1
  0.7 0.0 copy-start
  0.7 0.9 %copy-done = bf16[128,1024]{1,0:T(8,128)(2,1)S(1)} copy-done((bf16[128,1024]{1,0:T(8,128)(2,1)S(1)}, bf16[128,1024]{1,0:T(8,128)(2,1)}, u32[]{:S(2)}) %copy-start) | copy-done | bytes 262168
  1.6 0.4 shard_map.28
  2.1 37.1 %all_to_all.10 = bf16[128,2,1152]{2,1,0:T(2,128)(2,1)S(1)} all-to-all(bf16[128,2,1152]{2,1,0:T(2,128)(2,1)S(1)} %get-tuple-element.8), channel_id=1, replica_groups=mesh['z2'=2,'z1'=2,'z0'=2,'y2'=2,'y1'=2,'y0'=2,'core'=2,'far'=2,'near'=2..., dimensions={0} | all-to-all | bytes 1179648 | tf_op jit(solution)/shard_map/all_to_all | solution.py:177
  39.2 0.2 reshape.24.recv_ref
  39.4 0.1 slice.12
  39.5 3.6 %collective-permute-start.1 = (bf16[256,1024]{1,0:T(8,128)(2,1)S(1)}, bf16[256,1024]{1,0:T(8,128)(2,1)S(1)}, u32[]{:S(2)}, u32[]{:S(2)}) collective-permute-start(bf16[256,1024]{1,0:T(8,128)(2,1)S(1)} %slice.12), channel_id=1, source_target_pairs={{0,3},{1,2},{2,1},{3,0},{4,7},{5,6},{6,5},{7,4},{8,11},{9,10},{10,... | collective-permute-start | bytes 1572872 | tf_op jit(solution)/shard_map/ppermute | solution.py:169
  43.0 5.4 %collective-permute-start = (bf16[256,1024]{1,0:T(8,128)(2,1)S(1)}, bf16[256,1024]{1,0:T(8,128)(2,1)S(1)}, u32[]{:S(2)}, u32[]{:S(2)}) collective-permute-start(bf16[256,1024]{1,0:T(8,128)(2,1)S(1)} %slice.12), channel_id=1, source_target_pairs={{0,4},{4,0},{1,5},{5,1},{2,6},{6,2},{3,7},{7,3},{8,12},{12,8},{9,1... | collective-permute-start | bytes 1572872 | tf_op jit(solution)/shard_map/ppermute | solution.py:165
  48.4 0.1 slice_reduce_fusion
  48.5 1.9 %collective-permute-start.2 = (bf16[256]{0:T(256)(128)(2,1)S(1)}, bf16[256]{0:T(256)(128)(2,1)S(1)}, u32[]{:S(2)}, u32[]{:S(2)}) collective-permute-start(bf16[256]{0:T(256)(128)(2,1)S(1)} %slice_reduce_fusion), channel_id=1, source_target_pairs={{0,4},{4,0},{1,5},{5,1},{2,6},{6,2},{3,7},{7,3},{8,12},{12,8},{9,1... | collective-permute-start | bytes 1544 | tf_op jit(solution)/shard_map/ppermute | solution.py:165
  50.4 3.0 %collective-permute-start.3 = (bf16[256]{0:T(256)(128)(2,1)S(1)}, bf16[256]{0:T(256)(128)(2,1)S(1)}, u32[]{:S(2)}, u32[]{:S(2)}) collective-permute-start(bf16[256]{0:T(256)(128)(2,1)S(1)} %slice_reduce_fusion), channel_id=1, source_target_pairs={{0,3},{1,2},{2,1},{3,0},{4,7},{5,6},{6,5},{7,4},{8,11},{9,10},{10,... | collective-permute-start | bytes 1544 | tf_op jit(solution)/shard_map/ppermute | solution.py:169
  53.5 0.0 collective-permute-done.2
  53.5 2.8 %collective-permute-done.3 = bf16[256]{0:T(256)(128)(2,1)S(1)} collective-permute-done((bf16[256]{0:T(256)(128)(2,1)S(1)}, bf16[256]{0:T(256)(128)(2,1)S(1)}, u32[]{:S(2)}, u32[]{:S(2)}) %collective-permute-start.3) | collective-permute-done | bytes 544 | tf_op jit(solution)/shard_map/ppermute | solution.py:169
  56.3 0.0 collective-permute-done.1.beyond_ref
  56.3 0.0 collective-permute-done.twin_ref
  56.3 0.4 shard_map.30
  56.8 3.2 %collective-permute-start.4 = (f32[1,256]{1,0:T(1,128)S(1)}, f32[1,256]{1,0:T(1,128)S(1)}, u32[]{:S(2)}, u32[]{:S(2)}) collective-permute-start(f32[1,256]{1,0:T(1,128)S(1)} %shard_map.30), channel_id=1, source_target_pairs={{0,4},{4,0},{1,5},{5,1},{2,6},{6,2},{3,7},{7,3},{8,12},{12,8},{9,1... | collective-permute-start | bytes 3080 | tf_op jit(solution)/shard_map/ppermute | solution.py:165
  59.9 0.7 shard_map.29
  60.7 0.1 collective-permute-done.4
  60.8 0.1 reshape.27
  60.9 18.2 %all_to_all.11 = f32[128,1,2]{2,1,0:T(1,128)S(1)} all-to-all(f32[128,1,2]{2,1,0:T(1,128)S(1)} %bitcast.6), channel_id=1, replica_groups=mesh['z2'=2,'z1'=2,'z0'=2,'y2'=2,'y1'=2,'y0'=2,'core'=2,'far'=2,'near'=2..., dimensions={0} | all-to-all | bytes 2048 | tf_op jit(solution)/shard_map/all_to_all | solution.py:185
  79.1 0.6 shard_map.31
  (5 shorter events, 0.0 us)
Async XLA Ops:
  0.0 0.7 copy-start.1
  0.7 0.9 %copy-start = (bf16[128,1024]{1,0:T(8,128)(2,1)S(1)}, bf16[128,1024]{1,0:T(8,128)(2,1)}, u32[]{:S(2)}) copy-start(bf16[128,1024]{1,0:T(8,128)(2,1)} %emb_ref.1) | copy-start | bytes 786436
  39.5 16.9 %collective-permute-start.1 = (bf16[256,1024]{1,0:T(8,128)(2,1)S(1)}, bf16[256,1024]{1,0:T(8,128)(2,1)S(1)}, u32[]{:S(2)}, u32[]{:S(2)}) collective-permute-start(bf16[256,1024]{1,0:T(8,128)(2,1)S(1)} %slice.12), channel_id=1, source_target_pairs={{0,3},{1,2},{2,1},{3,0},{4,7},{5,6},{6,5},{7,4},{8,11},{9,10},{10,... | collective-permute-start | bytes 1572872 | tf_op jit(solution)/shard_map/ppermute | solution.py:169
  43.0 13.3 %collective-permute-start = (bf16[256,1024]{1,0:T(8,128)(2,1)S(1)}, bf16[256,1024]{1,0:T(8,128)(2,1)S(1)}, u32[]{:S(2)}, u32[]{:S(2)}) collective-permute-start(bf16[256,1024]{1,0:T(8,128)(2,1)S(1)} %slice.12), channel_id=1, source_target_pairs={{0,4},{4,0},{1,5},{5,1},{2,6},{6,2},{3,7},{7,3},{8,12},{12,8},{9,1... | collective-permute-start | bytes 1572872 | tf_op jit(solution)/shard_map/ppermute | solution.py:165
  48.5 5.0 %collective-permute-start.2 = (bf16[256]{0:T(256)(128)(2,1)S(1)}, bf16[256]{0:T(256)(128)(2,1)S(1)}, u32[]{:S(2)}, u32[]{:S(2)}) collective-permute-start(bf16[256]{0:T(256)(128)(2,1)S(1)} %slice_reduce_fusion), channel_id=1, source_target_pairs={{0,4},{4,0},{1,5},{5,1},{2,6},{6,2},{3,7},{7,3},{8,12},{12,8},{9,1... | collective-permute-start | bytes 1544 | tf_op jit(solution)/shard_map/ppermute | solution.py:165
  50.4 5.9 %collective-permute-start.3 = (bf16[256]{0:T(256)(128)(2,1)S(1)}, bf16[256]{0:T(256)(128)(2,1)S(1)}, u32[]{:S(2)}, u32[]{:S(2)}) collective-permute-start(bf16[256]{0:T(256)(128)(2,1)S(1)} %slice_reduce_fusion), channel_id=1, source_target_pairs={{0,3},{1,2},{2,1},{3,0},{4,7},{5,6},{6,5},{7,4},{8,11},{9,10},{10,... | collective-permute-start | bytes 1544 | tf_op jit(solution)/shard_map/ppermute | solution.py:169
  56.8 4.0 %collective-permute-start.4 = (f32[1,256]{1,0:T(1,128)S(1)}, f32[1,256]{1,0:T(1,128)S(1)}, u32[]{:S(2)}, u32[]{:S(2)}) collective-permute-start(f32[1,256]{1,0:T(1,128)S(1)} %shard_map.30), channel_id=1, source_target_pairs={{0,4},{4,0},{1,5},{5,1},{2,6},{6,2},{3,7},{7,3},{8,12},{12,8},{9,1... | collective-permute-start | bytes 3080 | tf_op jit(solution)/shard_map/ppermute | solution.py:165
